TPU v7x, 32 devices: a whole 2x2x4 slice. The times are simulated.
32 devices in a mesh: dp: 16 (over z, y, core), mp: 2 (over x).
Axes of the slice: x: 2, y: 2, z: 4, core: 2. Of those that a mesh axis runs over, the one named last changes fastest.
Arguments:
- tokens: bfloat16 [16384, 768], P('dp'), may hold values from -6 to 6
- document_lengths: int32 [1, 8], replicated, may hold values from 0 to 16384, as said below
- feature_maps: bfloat16 [12, 64, 256], replicated, may hold values from -5 to 5
- joint_weight: bfloat16 [768, 2304], P(('dp', 'mp')), may hold values from -0.21875 to 0.21875
- joint_bias: bfloat16 [2304], P(('dp', 'mp')), may hold values from -1.25 to 1.25
- output_weight: bfloat16 [768, 768], P(('dp', 'mp')), may hold values from -1.75 to 1.75
- output_bias: bfloat16 [768], P(('dp', 'mp')), may hold values from -1.25 to 1.25
- first_gain: bfloat16 [768], P(('dp', 'mp')), may hold values from 0.25 to 1.75
- first_shift: bfloat16 [768], P(('dp', 'mp')), may hold values from -1.25 to 1.25
- up_weight: bfloat16 [768, 3072], P(None, 'mp'), may hold values from -0.21875 to 0.21875
- up_bias: bfloat16 [3072], P('mp'), may hold values from -1.25 to 1.25
- down_weight: bfloat16 [3072, 768], P('mp'), may hold values from -0.109375 to 0.109375
- down_bias: bfloat16 [768], replicated, may hold values from -1.25 to 1.25
- second_gain: bfloat16 [768], P(('dp', 'mp')), may hold values from 0.25 to 1.75
- second_shift: bfloat16 [768], P(('dp', 'mp')), may hold values from -1.25 to 1.25
- cotangent: bfloat16 [16384, 768], P('dp'), may hold values from -6 to 6
Outputs:
- layer_output: bfloat16 [16384, 768], P('dp')
- tokens_grad: bfloat16 [16384, 768], P('dp')
- joint_weight_grad: float32 [768, 2304], P(('dp', 'mp'))
- joint_bias_grad: float32 [2304], P(('dp', 'mp'))
- output_weight_grad: float32 [768, 768], P(('dp', 'mp'))
- output_bias_grad: float32 [768], P(('dp', 'mp'))
- first_gain_grad: float32 [768], P(('dp', 'mp'))
- first_shift_grad: float32 [768], P(('dp', 'mp'))
- up_weight_grad: float32 [768, 3072], P(None, 'mp')
- up_bias_grad: float32 [3072], P('mp')
- down_weight_grad: float32 [3072, 768], P('mp')
- down_bias_grad: float32 [768], replicated
- second_gain_grad: float32 [768], P(('dp', 'mp'))
- second_shift_grad: float32 [768], P(('dp', 'mp'))
Inputs may be any that keep to these rules, and one draw needn't show every extreme that they name: `document_lengths`: each row of 16384 positions holds its 8 documents in order from its first position, then padding. In every row one document has more than 15360 tokens and the others together with the padding fewer than 1024.
All inputs are finite; a program needn't handle non-finite values.
Results may differ from a plain program's by a relative error of at most 0.033.
Values may be sent and summed in bfloat16 or wider, within the bound.
No kernel may reach another device: no remote copies, remote signals or barrier semaphores. Data moves between devices by JAX's collectives and lax.ppermute only.
A program may use at most 576 MiB of HBM per device.

v0:
```python
from functools import partial
import math

import jax
import jax.numpy as jnp
from jax import lax
from jax.sharding import PartitionSpec as P

EPSILON = 1e-05
HIGHEST = lax.Precision.HIGHEST


def entering(array, axis, join, neutral, backward):
    count = lax.axis_size(axis)
    place = lax.axis_index(axis)
    ahead = count - 1 - place if backward else place
    gathered = jax.tree.map(
        lambda a, kind: lax.all_gather(a.astype(kind), axis),
        array,
        jax.tree.map(lambda a: jnp.bfloat16 if a.dtype == jnp.float32 else a.dtype, array),
    )
    state = jax.tree.map(lambda a, e: jnp.zeros_like(a) + jnp.asarray(e, a.dtype), array, neutral)

    def one(turn, state):
        source = count - 1 - turn if backward else turn
        return join(
            state,
            jax.tree.map(
                lambda a, own: lax.dynamic_index_in_dim(a, source, 0, False).astype(own.dtype),
                gathered,
                array,
            ),
        )

    return lax.fori_loop(0, ahead, one, state)


def normalize(values):
    average = jnp.mean(values, axis=-1, keepdims=True)
    centered = values - average
    inverse = lax.rsqrt(jnp.mean(centered * centered, axis=-1, keepdims=True) + EPSILON)
    return (centered * inverse, inverse)


def norm_backward(normed_grad, normed, inverse):
    first_term = jnp.mean(normed_grad, axis=-1, keepdims=True)
    second_term = jnp.mean(normed_grad * normed, axis=-1, keepdims=True)
    return inverse * (normed_grad - first_term - normed * second_term)


def feature_map(unscaled, feature_maps):
    scaled = unscaled * unscaled.shape[-1] ** (-0.25)
    projected = jnp.einsum(
        "thd,hdf->thf",
        scaled.astype(jnp.bfloat16),
        feature_maps,
        preferred_element_type=jnp.float32,
    )
    positive = jnp.exp(
        projected - 0.5 * jnp.sum(scaled * scaled, axis=-1, keepdims=True)
    ) / math.sqrt(feature_maps.shape[-1])
    return (scaled, positive)


def feature_backward(positive_grad, positive, scaled, feature_maps):
    exponent_grad = positive_grad * positive
    projected_grad = exponent_grad.astype(jnp.bfloat16)
    scaled_grad = jnp.einsum(
        "thf,hdf->thd", projected_grad, feature_maps, preferred_element_type=jnp.float32
    )
    scaled_grad = scaled_grad - scaled * jnp.sum(exponent_grad, axis=-1, keepdims=True)
    return scaled_grad * scaled.shape[-1] ** (-0.25)


def join_marks(lower_marks, upper_marks, joined):
    lower_alive = lower_marks[3]
    upper_alive = upper_marks[3]
    opening = jnp.where(lower_alive > 0.5, lower_marks[0], upper_marks[0])
    closing = jnp.where(upper_alive > 0.5, upper_marks[1], lower_marks[1])
    single = jnp.where(
        lower_alive * upper_alive > 0.5,
        lower_marks[2] * upper_marks[2] * joined,
        lower_marks[2] * lower_alive + upper_marks[2] * upper_alive,
    )
    return jnp.stack([opening, closing, single, jnp.maximum(lower_alive, upper_alive)])


def forward_join(lower_part, upper_part):
    lower_marks, lower_moments, lower_masses = lower_part
    upper_marks, upper_moments, upper_masses = upper_part
    joined = (lower_marks[1] == upper_marks[0]).astype(jnp.float32)
    linked = upper_marks[2] * joined * lower_marks[3]
    moments = jnp.where(upper_marks[3] > 0.5, upper_moments + linked * lower_moments, lower_moments)
    masses = jnp.where(upper_marks[3] > 0.5, upper_masses + linked * lower_masses, lower_masses)
    return (join_marks(lower_marks, upper_marks, joined), moments, masses)


def backward_join(upper_part, lower_part):
    lower_marks, lower_moments, lower_masses = lower_part
    upper_marks, upper_moments, upper_masses = upper_part
    joined = (lower_marks[1] == upper_marks[0]).astype(jnp.float32)
    linked = lower_marks[2] * joined * upper_marks[3]
    moments = jnp.where(lower_marks[3] > 0.5, lower_moments + linked * upper_moments, upper_moments)
    masses = jnp.where(lower_marks[3] > 0.5, lower_masses + linked * upper_masses, upper_masses)
    return (join_marks(lower_marks, upper_marks, joined), moments, masses)


def boundary_runs(trailing, leading):
    empty_tail = tuple((jnp.zeros_like(member) for member in trailing))
    before = entering(
        (trailing[0], trailing[1], trailing[2]), "dp", forward_join, empty_tail, False
    )
    following = entering(
        (leading[0], leading[1], leading[2]), "dp", backward_join, empty_tail, True
    )
    return (before, following)


def segment_totals(moments, masses, markers, first_pick, final_pick):
    head_count, feature_count, slot_count, head_size = moments.shape
    tail_moments = jnp.sum(moments * final_pick[None, None, :, None], axis=2).reshape(
        head_count, feature_count * head_size
    )
    tail_masses = jnp.sum(masses * final_pick[None, None, :], axis=2)
    lead_moments = jnp.sum(moments * first_pick[None, None, :, None], axis=2).reshape(
        head_count, feature_count * head_size
    )
    lead_masses = jnp.sum(masses * first_pick[None, None, :], axis=2)
    before, following = boundary_runs(
        (markers, tail_moments, tail_masses), (markers, lead_moments, lead_masses)
    )
    take_before = before[0][3] * (before[0][1] == markers[0]).astype(jnp.float32)
    take_after = following[0][3] * (following[0][0] == markers[1]).astype(jnp.float32)
    lower_pick = take_before * first_pick
    upper_pick = take_after * final_pick
    moments = (
        moments
        + lower_pick[None, None, :, None]
        * before[1].reshape(head_count, feature_count, 1, head_size)
        + upper_pick[None, None, :, None]
        * following[1].reshape(head_count, feature_count, 1, head_size)
    )
    masses = (
        masses
        + lower_pick[None, None, :] * before[2][:, :, None]
        + upper_pick[None, None, :] * following[2][:, :, None]
    )
    return (moments, masses)


def local(
    tokens,
    document_lengths,
    feature_maps,
    joint_weight,
    joint_bias,
    output_weight,
    output_bias,
    first_gain,
    first_shift,
    up_weight,
    up_bias,
    down_weight,
    down_bias,
    second_gain,
    second_shift,
    cotangent,
):
    gathered = (
        lax.all_gather(joint_weight, ("dp", "mp"), axis=0, tiled=True),
        lax.all_gather(joint_bias, ("dp", "mp"), axis=0, tiled=True),
        lax.all_gather(output_weight, ("dp", "mp"), axis=0, tiled=True),
        lax.all_gather(output_bias, ("dp", "mp"), axis=0, tiled=True),
        lax.all_gather(first_gain, ("dp", "mp"), axis=0, tiled=True),
        lax.all_gather(first_shift, ("dp", "mp"), axis=0, tiled=True),
        lax.all_gather(second_gain, ("dp", "mp"), axis=0, tiled=True),
        lax.all_gather(second_shift, ("dp", "mp"), axis=0, tiled=True),
    )
    (
        joint_full,
        joint_offset,
        output_full,
        output_offset,
        gain_first,
        shift_first,
        gain_second,
        shift_second,
    ) = gathered
    tok_rows, model_width = tokens.shape
    head_count, head_size, feature_count = feature_maps.shape
    row_count, slot_count = document_lengths.shape
    model_rank = lax.axis_index("mp")
    model_count = lax.axis_size("mp")
    rank_index = lax.axis_index("dp")
    row_tokens = tok_rows * lax.axis_size("dp") // row_count
    row_number = rank_index * tok_rows // row_tokens
    inner_place = (
        rank_index * tok_rows - row_number * row_tokens + jnp.arange(tok_rows, dtype=jnp.int32)
    )
    row_ends_all = jnp.cumsum(document_lengths, axis=1)
    row_pick = (jnp.arange(row_count, dtype=jnp.int32) == row_number).astype(jnp.int32)
    row_ends = jnp.sum(row_ends_all * row_pick[:, None], axis=0)
    document = jnp.sum((row_ends[None, :] <= inner_place[:, None]).astype(jnp.int32), axis=1)
    segment = (row_number * (slot_count + 1) + document).astype(jnp.float32)
    onehot = (document[:, None] == jnp.arange(slot_count, dtype=jnp.int32)[None, :]).astype(
        jnp.float32
    )
    onehot_low = onehot.astype(jnp.bfloat16)
    live_mask = jnp.sum(onehot, axis=1)
    first_pick = onehot[0]
    final_pick = onehot[-1]
    markers = jnp.stack(
        [
            segment[0],
            segment[-1],
            (segment[0] == segment[-1]).astype(jnp.float32),
            jnp.ones((), jnp.float32),
        ]
    )
    joint_value = jnp.dot(
        tokens, joint_full, preferred_element_type=jnp.float32
    ) + joint_offset.astype(jnp.float32)
    query_raw = joint_value[:, :model_width].reshape(tok_rows, head_count, head_size)
    key_raw = joint_value[:, model_width : 2 * model_width].reshape(tok_rows, head_count, head_size)
    values_low = (
        joint_value[:, 2 * model_width :]
        .astype(jnp.bfloat16)
        .reshape(tok_rows, head_count, head_size)
    )
    query_scaled, query_positive = feature_map(query_raw, feature_maps)
    key_scaled, key_positive = feature_map(key_raw, feature_maps)
    query_low = query_positive.astype(jnp.bfloat16)
    key_low = key_positive.astype(jnp.bfloat16)
    query_wide = query_low.astype(jnp.float32)
    spread_values = onehot_low[:, :, None, None] * values_low[:, None, :, :]
    local_moments = jnp.einsum(
        "thf,tdhe->hfde", key_low, spread_values, preferred_element_type=jnp.float32
    )
    local_masses = jnp.einsum(
        "td,thf->hfd", onehot_low, key_low, preferred_element_type=jnp.float32
    )
    moments_total, masses_total = segment_totals(
        local_moments, local_masses, markers, first_pick, final_pick
    )
    moments_low = moments_total.astype(jnp.bfloat16)
    spread = jnp.einsum(
        "thf,hfde->thde", query_low, moments_low, preferred_element_type=jnp.float32
    )
    numerator = jnp.sum(spread * onehot[:, None, :, None], axis=2)
    mass_query = jnp.einsum("thf,hfd->thd", query_wide, masses_total, precision=HIGHEST)
    denominator = jnp.sum(mass_query * onehot[:, None, :], axis=2)
    safe_total = jnp.where(live_mask[:, None] > 0.5, denominator, 1.0)
    attention = numerator / safe_total[:, :, None] * live_mask[:, None, None]
    attention_low = attention.reshape(tok_rows, model_width).astype(jnp.bfloat16)
    branch = jnp.dot(
        attention_low, output_full, preferred_element_type=jnp.float32
    ) + output_offset.astype(jnp.float32)
    first_normed, first_inverse = normalize(tokens.astype(jnp.float32) + branch)
    hidden = first_normed * gain_first.astype(jnp.float32) + shift_first.astype(jnp.float32)
    hidden_low = hidden.astype(jnp.bfloat16)
    up_value = jnp.dot(hidden_low, up_weight, preferred_element_type=jnp.float32) + up_bias.astype(
        jnp.float32
    )
    gelu_value, gelu_pullback = jax.vjp(partial(jax.nn.gelu, approximate=False), up_value)
    active = gelu_value.astype(jnp.bfloat16)
    partial_out = jnp.dot(active, down_weight, preferred_element_type=jnp.float32)
    feedforward = lax.psum(partial_out.astype(jnp.bfloat16), "mp").astype(
        jnp.float32
    ) + down_bias.astype(jnp.float32)
    second_normed, second_inverse = normalize(hidden + feedforward)
    layer_output = (
        second_normed * gain_second.astype(jnp.float32) + shift_second.astype(jnp.float32)
    ).astype(jnp.bfloat16)
    output_cot = cotangent.astype(jnp.float32)
    shift_second_grad = jnp.sum(output_cot, axis=0)
    gain_second_grad = jnp.sum(output_cot * second_normed, axis=0)
    second_residual = norm_backward(
        output_cot * gain_second.astype(jnp.float32), second_normed, second_inverse
    )
    feedforward_low = second_residual.astype(jnp.bfloat16)
    down_bias_grad = jnp.sum(feedforward_low.astype(jnp.float32), axis=0)
    down_weight_grad = jnp.einsum(
        "tk,td->kd", active, feedforward_low, preferred_element_type=jnp.float32
    )
    active_grad = jnp.einsum(
        "td,kd->tk", feedforward_low, down_weight, preferred_element_type=jnp.float32
    )
    up_grad_low = gelu_pullback(active_grad)[0].astype(jnp.bfloat16)
    up_bias_grad = jnp.sum(up_grad_low.astype(jnp.float32), axis=0)
    up_weight_grad = jnp.einsum(
        "td,tk->dk", hidden_low, up_grad_low, preferred_element_type=jnp.float32
    )
    hidden_part = jnp.einsum(
        "tk,dk->td", up_grad_low, up_weight, preferred_element_type=jnp.float32
    )
    hidden_grad = second_residual + lax.psum(hidden_part.astype(jnp.bfloat16), "mp").astype(
        jnp.float32
    )
    shift_first_grad = jnp.sum(hidden_grad, axis=0)
    gain_first_grad = jnp.sum(hidden_grad * first_normed, axis=0)
    first_residual = norm_backward(
        hidden_grad * gain_first.astype(jnp.float32), first_normed, first_inverse
    )
    branch_low = first_residual.astype(jnp.bfloat16)
    output_offset_grad = jnp.sum(branch_low.astype(jnp.float32), axis=0)
    output_weight_grad = jnp.einsum(
        "tj,td->jd", attention_low, branch_low, preferred_element_type=jnp.float32
    )
    attention_grad = jnp.einsum(
        "td,jd->tj", branch_low, output_full, preferred_element_type=jnp.float32
    ).reshape(tok_rows, head_count, head_size)
    numerator_low = (attention_grad * live_mask[:, None, None] / safe_total[:, :, None]).astype(
        jnp.bfloat16
    )
    safe_grad = -jnp.sum(attention_grad * attention, axis=-1) / safe_total
    denominator_grad = jnp.where(live_mask[:, None] > 0.5, safe_grad, 0.0)
    spread_grad = onehot_low[:, None, :, None] * numerator_low[:, :, None, :]
    mass_part = denominator_grad[:, :, None] * onehot[:, None, :]
    query_grad = jnp.einsum(
        "thde,hfde->thf", spread_grad, moments_low, preferred_element_type=jnp.float32
    )
    query_grad = query_grad + jnp.einsum("thd,hfd->thf", mass_part, masses_total, precision=HIGHEST)
    local_moment_grads = jnp.einsum(
        "thf,thde->hfde", query_low, spread_grad, preferred_element_type=jnp.float32
    )
    local_mass_grads = jnp.einsum("thf,thd->hfd", query_wide, mass_part, precision=HIGHEST)
    moment_grads, mass_grads = segment_totals(
        local_moment_grads, local_mass_grads, markers, first_pick, final_pick
    )
    moment_grads_low = moment_grads.astype(jnp.bfloat16)
    key_grad = jnp.einsum(
        "tdhe,hfde->thf", spread_values, moment_grads_low, preferred_element_type=jnp.float32
    )
    key_grad = key_grad + jnp.einsum("td,hfd->thf", onehot, mass_grads, precision=HIGHEST)
    value_spread = jnp.einsum(
        "thf,hfde->thde", key_low, moment_grads_low, preferred_element_type=jnp.float32
    )
    value_grad = jnp.sum(value_spread * onehot[:, None, :, None], axis=2)
    query_raw_grad = feature_backward(query_grad, query_positive, query_scaled, feature_maps)
    key_raw_grad = feature_backward(key_grad, key_positive, key_scaled, feature_maps)
    joint_grad_low = jnp.concatenate(
        [
            query_raw_grad.reshape(tok_rows, model_width),
            key_raw_grad.reshape(tok_rows, model_width),
            value_grad.reshape(tok_rows, model_width),
        ],
        axis=1,
    ).astype(jnp.bfloat16)
    joint_offset_grad = jnp.sum(joint_grad_low.astype(jnp.float32), axis=0)
    joint_weight_grad = jnp.einsum(
        "tj,tk->jk", tokens, joint_grad_low, preferred_element_type=jnp.float32
    )
    joint_back = jnp.einsum(
        "tk,jk->tj", joint_grad_low, joint_full, preferred_element_type=jnp.float32
    )
    tokens_grad = (first_residual + joint_back).astype(jnp.bfloat16)
    feedforward_sums = lax.psum(
        (up_weight_grad, up_bias_grad, down_weight_grad, down_bias_grad), "dp"
    )
    attention_sums = (
        lax.psum_scatter(joint_weight_grad, "dp", scatter_dimension=0, tiled=True),
        lax.psum_scatter(joint_offset_grad, "dp", scatter_dimension=0, tiled=True),
        lax.psum_scatter(output_weight_grad, "dp", scatter_dimension=0, tiled=True),
        lax.psum_scatter(output_offset_grad, "dp", scatter_dimension=0, tiled=True),
        lax.psum_scatter(gain_first_grad, "dp", scatter_dimension=0, tiled=True),
        lax.psum_scatter(shift_first_grad, "dp", scatter_dimension=0, tiled=True),
        lax.psum_scatter(gain_second_grad, "dp", scatter_dimension=0, tiled=True),
        lax.psum_scatter(shift_second_grad, "dp", scatter_dimension=0, tiled=True),
    )

    def keep_share(member):
        share_rows = member.shape[0] // model_count
        return lax.dynamic_slice_in_dim(member, model_rank * share_rows, share_rows, 0)

    owned = [keep_share(member) for member in attention_sums]
    return (
        layer_output,
        tokens_grad,
        owned[0],
        owned[1],
        owned[2],
        owned[3],
        owned[4],
        owned[5],
        feedforward_sums[0],
        feedforward_sums[1],
        feedforward_sums[2],
        feedforward_sums[3],
        owned[6],
        owned[7],
    )


def solution(mesh):
    in_specs = (
        P("dp", None),
        P(),
        P(),
        P(("dp", "mp"), None),
        P(("dp", "mp")),
        P(("dp", "mp"), None),
        P(("dp", "mp")),
        P(("dp", "mp")),
        P(("dp", "mp")),
        P(None, "mp"),
        P("mp"),
        P("mp", None),
        P(),
        P(("dp", "mp")),
        P(("dp", "mp")),
        P("dp", None),
    )
    out_specs = (
        P("dp", None),
        P("dp", None),
        P(("dp", "mp"), None),
        P(("dp", "mp")),
        P(("dp", "mp"), None),
        P(("dp", "mp")),
        P(("dp", "mp")),
        P(("dp", "mp")),
        P(None, "mp"),
        P("mp"),
        P("mp", None),
        P(),
        P(("dp", "mp")),
        P(("dp", "mp")),
    )
    return jax.shard_map(local, mesh=mesh, in_specs=in_specs, out_specs=out_specs, check_vma=False)
```

profile of v0, /device:TPU:0, one launch (start us, length us, event | category | flops | bytes accessed | tf_op | source)
XLA Modules:
  0.0 1483.1 jit_solution(5476030310125373995)
XLA Ops:
  13.9 42.5 %all-reduce.14 = (bf16[2304]{0:T(1024)(128)(2,1)S(1)}, bf16[768]{0:T(1024)(128)(2,1)S(1)}, bf16[768]{0:T(1024)(128)(2,1)}, bf16[768]{0:T(1024)(128)(2,1)}, bf16[...) all-reduce(bf16[2304]{0:T(1024)(128)(2,1)S(1)} %dynamic-update-slice, ...), channel_id=1, replica_groups=mesh['dp'=16,'mp'=2] {'dp','mp'}, use_global_device_ids=true, to_apply=%add | all-reduce | flops 6144 | bytes 24576
  57.3 16.8 %all-gather.16.cloned.1.call-done = bf16[768,2304]{1,0:T(8,128)(2,1)} async-done(((bf16[24,2304]{1,0:T(8,128)(2,1)}), bf16[768,2304]{1,0:T(8,128)(2,1)}) %all-gather.16.cloned.1.call-update) | async-done | bytes 3538960 | tf_op jit(solution)/shard_map/all_gather | solution.py:170
  93.4 10.0 fusion.19
  103.5 10.1 multiply_reduce_fusion.3
  126.3 20.1 %all-gather.4 = bf16[16,1,4]{2,1,0:T(2,128)(2,1)S(1)} all-gather(bf16[1,1,4]{2,1,0:T(2,128)(2,1)S(1)} %maximum_bitcast_fusion), channel_id=1, replica_groups=mesh['dp'=16,'mp'=2] {'dp'}, dimensions={0}, use_global_device_ids=true | all-gather | bytes 136 | tf_op jit(solution)/shard_map/all_gather | solution.py:18
  155.5 19.9 %all-gather.5 = bf16[16,12,256]{2,1,0:T(8,128)(2,1)} all-gather(bf16[1,12,256]{2,1,0:T(8,128)(2,1)S(1)} %bitcast.369), channel_id=2, replica_groups=mesh['dp'=16,'mp'=2] {'dp'}, dimensions={0}, use_global_device_ids=true | all-gather | bytes 104448 | tf_op jit(solution)/shard_map/all_gather | solution.py:18
  175.5 20.7 %all-gather.6 = bf16[16,12,256]{2,1,0:T(8,128)(2,1)} all-gather(bf16[1,12,256]{2,1,0:T(8,128)(2,1)S(1)} %bitcast.367), channel_id=3, replica_groups=mesh['dp'=16,'mp'=2] {'dp'}, dimensions={0}, use_global_device_ids=true | all-gather | bytes 104448 | tf_op jit(solution)/shard_map/all_gather | solution.py:18
  202.9 7.8 fusion.20
  212.7 54.7 %all-gather.20.cloned.1.call-done = bf16[16,12,16384]{2,1,0:T(8,128)(2,1)} async-done(((bf16[1,12,16384]{2,1,0:T(8,128)(2,1)}), bf16[16,12,16384]{2,1,0:T(8,128)(2,1)}) %all-gather.20.cloned.1.call-update) | async-done | bytes 6291472 | tf_op jit(solution)/shard_map/all_gather | solution.py:18
  268.5 251.0 %while.61 = (s32[]{:T(128)}, f32[4]{0:T(128)S(1)}, f32[12,16384]{1,0:T(8,128)}, f32[12,256]{1,0:T(8,128)S(1)}, s32[]{:T(128)}, /*index=5*/bf16[16,4]{0,1:T(4,128...) while((s32[]{:T(128)}, f32[4]{0:T(128)S(1)}, ...), condition=%wide.region_10.11_spmd, body=%wide.region_9.10_spmd.sunk | while | flops 798758 | bytes 1997306 | solution.py:35
  539.1 10.4 fusion.9
  557.7 19.0 %multiply_convert_fusion = (bf16[1024,1536]{1,0:T(8,128)(2,1)S(1)}, f32[1024,1536]{1,0:T(8,128)}, f32[1024,1536]{1,0:T(8,128)}) fusion(f32[1536]{0:T(1024)S(1)} %copy-done.58, bf16[768,1536]{1,0:T(8,128)(2,1)S(1)} %copy-done, f32[1024,768]{0,1:T(8,128)S(1)} %get-tuple-element.577, f32[768]{0:T(1024)S(1)} %copy-done.46, f32[768]{0:T(1024)S(1)} %convert_element_type.382, ...), kind=kOutput, calls=%fused_computation.61 | convolution fusion | flops 2523660288 | bytes 21254144 | tf_op jit(solution)/shard_map/dot_general | solution.py:261
  585.1 46.0 %all-reduce.19.cloned.1.call-done = bf16[1024,768]{0,1:T(8,128)(2,1)} async-done(((bf16[1024,768]{0,1:T(8,128)(2,1)}), bf16[1024,768]{0,1:T(8,128)(2,1)}) %all-reduce.19.cloned.1.call-update) | async-done | bytes 1572880 | tf_op jit(solution)/shard_map/psum | solution.py:267
  640.8 7.8 convert_reduce_fusion.1
  654.2 51.6 %all-reduce.21.cloned.1.call-done = bf16[1024,768]{0,1:T(8,128)(2,1)} async-done(((bf16[1024,768]{0,1:T(8,128)(2,1)}), bf16[1024,768]{0,1:T(8,128)(2,1)}) %all-reduce.21.cloned.1.call-update) | async-done | bytes 1572880 | tf_op jit(solution)/shard_map/psum | solution.py:296
  705.8 7.4 multiply_reduce_fusion.4
  723.8 12.5 fusion.125
  744.0 7.2 multiply_reduce_fusion.13
  751.2 22.5 %all-gather.7 = bf16[16,12,256]{2,1,0:T(8,128)(2,1)S(1)} all-gather(bf16[1,12,256]{2,1,0:T(8,128)(2,1)S(1)} %bitcast.368), channel_id=4, replica_groups=mesh['dp'=16,'mp'=2] {'dp'}, dimensions={0}, use_global_device_ids=true | all-gather | bytes 104448 | tf_op jit(solution)/shard_map/all_gather | solution.py:18
  773.7 18.4 %all-gather.8 = bf16[16,12,256]{2,1,0:T(8,128)(2,1)S(1)} all-gather(bf16[1,12,256]{2,1,0:T(8,128)(2,1)S(1)} %bitcast.366), channel_id=5, replica_groups=mesh['dp'=16,'mp'=2] {'dp'}, dimensions={0}, use_global_device_ids=true | all-gather | bytes 104448 | tf_op jit(solution)/shard_map/all_gather | solution.py:18
  792.1 10.7 fusion.61
  802.8 18.6 %fusion.124 = (f32[1024,12]{0,1:T(8,128)S(1)}, bf16[1024,12,256]{0,2,1:T(8,128)(2,1)}) fusion(f32[1024,12]{0,1:T(8,128)S(1)} %copy-done.37, f32[12,1024,256]{1,2,0:T(8,128)} %get-tuple-element.575, f32[1024,12]{0,1:T(8,128)S(1)} %divide_select_fusion, f32[1024,8]{0,1:T(8,128)S(1)} %copy-done.29, f32[12,256,8]{1,2,0:T(8,128)S(1)} %copy-done.27, ...), kind=kOutput, calls=%fused_computation.231 | convolution fusion | flops 321048576 | bytes 31760448 | tf_op jit(solution)/shard_map/thd,hfd->thf/dot_general | solution.py:322
  837.5 56.4 %all-gather.26.cloned.1.call-done = bf16[16,12,16384]{2,1,0:T(8,128)(2,1)} async-done(((bf16[1,12,16384]{2,1,0:T(8,128)(2,1)}), bf16[16,12,16384]{2,1,0:T(8,128)(2,1)}) %all-gather.26.cloned.1.call-update) | async-done | bytes 6291472 | tf_op jit(solution)/shard_map/all_gather | solution.py:18
  893.9 238.0 %while.63 = (s32[]{:T(128)}, f32[4]{0:T(128)S(1)}, f32[12,16384]{1,0:T(8,128)S(1)}, f32[12,256]{1,0:T(8,128)S(1)}, s32[]{:T(128)}, /*index=5*/bf16[16,4]{0,1:T(4...) while((s32[]{:T(128)}, f32[4]{0:T(128)S(1)}, ...), condition=%wide.region_34.35_spmd, body=%wide.region_33.34_spmd.sunk | while | flops 798758 | bytes 1997306 | solution.py:35
  1138.1 10.8 fusion.10
  1148.9 13.3 fusion.123
  1164.6 9.9 fusion.8
  1174.5 9.1 convolution_bitcast_fusion
  1183.6 8.0 copy.242
  1213.6 61.0 %all-reduce.12 = (f32[2304]{0:T(1024)S(1)}, f32[768]{0:T(1024)S(1)}, f32[768]{0:T(1024)S(1)}, f32[768]{0:T(1024)S(1)}, f32[1536]{0:T(1024)}, /*index=5*/f32[768]{0:T(1024)}, f32[768]{0:T(1024)S(1)}, f32[768]{0:T(1024)S(1)}) all-reduce(f32[2304]{0:T(1024)S(1)} %convert_reduce_fusion, ...), channel_id=7, replica_groups=mesh['dp'=16,'mp'=2] {'dp'}, use_global_device_ids=true, to_apply=%region_39.40.clone | all-reduce | flops 8448 | bytes 67584
  1277.6 8.9 add_convert_fusion.3
  1291.3 177.7 %all-reduce.23.cloned.1.call-done = (f32[768,1536]{1,0:T(8,128)}, f32[1536,768]{1,0:T(8,128)}) async-done(((f32[768,1536]{1,0:T(8,128)}, f32[1536,768]{1,0:T(8,128)}), (f32[768,1536]{1,0:T(8,128)}, f32[1536,768]{1,0:T(8,128)})) %all-reduce.23.cloned.1.call-update) | async-done | bytes 9437200 | tf_op jit(solution)/shard_map/psum | solution.py:357
  (491 shorter events, 288.7 us)
Async XLA Ops:
  7.2 550.5 %copy-start = (bf16[768,1536]{1,0:T(8,128)(2,1)S(1)}, bf16[768,1536]{1,0:T(8,128)(2,1)}, u32[]{:S(2)}) copy-start(bf16[768,1536]{1,0:T(8,128)(2,1)} %param.33) | copy-start | bytes 7077892
  7.2 66.9 %all-gather.16.cloned.1.call-start = ((), (), s32[]{:S(2)}) async-start(), calls=%async_computation.2 | async-start | bytes 3649536 | tf_op jit(solution)/shard_map/all_gather | solution.py:170
  7.9 202.7 %all-gather.18.cloned.1.call-start = ((), (), s32[]{:S(2)}) async-start(), calls=%async_computation.3 | async-start | bytes 8912896 | tf_op jit(solution)/shard_map/all_gather | solution.py:18
  56.5 94.5 %copy-start.42 = (s32[1024]{0:T(1024)}, s32[1024]{0:T(1024)S(1)}, u32[]{:S(2)}) copy-start(s32[1024]{0:T(1024)S(1)} %convert_reduce_fusion.5) | copy-start | bytes 12292
  56.5 47.0 %copy-start.44 = (bf16[1024,8]{0,1:T(8,128)(2,1)}, bf16[1024,8]{0,1:T(8,128)(2,1)S(1)}, u32[]{:S(2)}) copy-start(bf16[1024,8]{0,1:T(8,128)(2,1)S(1)} %get-tuple-element.560) | copy-start | bytes 49156
  57.3 46.2 %copy-start.53 = (f32[8]{0:T(128)}, f32[8]{0:T(128)S(1)}, u32[]{:S(2)}) copy-start(f32[8]{0:T(128)S(1)} %get-tuple-element.428) | copy-start | bytes 100
  57.3 46.2 %copy-start.55 = (f32[8]{0:T(128)}, f32[8]{0:T(128)S(1)}, u32[]{:S(2)}) copy-start(f32[8]{0:T(128)S(1)} %get-tuple-element.429) | copy-start | bytes 100
  90.8 12.6 copy-start.34
  116.4 151.0 %all-gather.20.cloned.1.call-start = ((), (), s32[]{:S(2)}) async-start(), calls=%async_computation.4 | async-start | bytes 8912896 | tf_op jit(solution)/shard_map/all_gather | solution.py:18
  119.7 433.6 %all-gather.22.cloned.1.call-start = ((), (), s32[]{:S(2)}) async-start(), calls=%async_computation.5 | async-start | bytes 1216512 | tf_op jit(solution)/shard_map/all_gather | solution.py:172
  120.3 510.8 %all-reduce.19.cloned.1.call-start = ((), (), s32[]{:S(2)}) async-start(), calls=%async_computation.6 | async-start | bytes 3145728 | tf_op jit(solution)/shard_map/psum | solution.py:267
  155.5 367.8 %copy-start.26 = (f32[12,256,8]{1,2,0:T(8,128)}, f32[12,256,8]{1,2,0:T(8,128)S(1)}, u32[]{:S(2)}) copy-start(f32[12,256,8]{1,2,0:T(8,128)S(1)} %get-tuple-element.573) | copy-start | bytes 294916
  210.8 312.5 %copy-start.18 = (f32[12,256]{1,0:T(8,128)}, f32[12,256]{1,0:T(8,128)S(1)}, u32[]{:S(2)}) copy-start(f32[12,256]{1,0:T(8,128)S(1)} %get-tuple-element.320) | copy-start | bytes 36868
  533.0 16.4 %copy-start.30 = (f32[12,256,64]{1,2,0:T(8,128)}, f32[12,256,64]{1,2,0:T(8,128)S(1)}, u32[]{:S(2)}) copy-start(f32[12,256,64]{1,2,0:T(8,128)S(1)} %copy.200) | copy-start | bytes 2359300
  557.2 19.5 %copy-start.3 = (f32[1024,768]{0,1:T(8,128)}, f32[1024,768]{0,1:T(8,128)S(1)}, u32[]{:S(2)}) copy-start(f32[1024,768]{0,1:T(8,128)S(1)} %get-tuple-element.577) | copy-start | bytes 9437188
  557.7 20.7 %copy-start.68 = (bf16[1536,768]{1,0:T(8,128)(2,1)S(1)}, bf16[1536,768]{1,0:T(8,128)(2,1)}, u32[]{:S(2)}) copy-start(bf16[1536,768]{1,0:T(8,128)(2,1)} %param.35) | copy-start | bytes 7077892
  582.2 123.5 %all-reduce.21.cloned.1.call-start = ((), (), s32[]{:S(2)}) async-start(), calls=%async_computation.7 | async-start | bytes 3145728 | tf_op jit(solution)/shard_map/psum | solution.py:296
  654.1 176.8 %all-gather.24.cloned.1.call-start = ((), (), s32[]{:S(2)}) async-start(), calls=%async_computation.8 | async-start | bytes 8912896 | tf_op jit(solution)/shard_map/all_gather | solution.py:18
  723.8 12.5 copy-start.54
  723.8 12.5 copy-start.56
  741.9 151.9 %all-gather.26.cloned.1.call-start = ((), (), s32[]{:S(2)}) async-start(), calls=%async_computation.9 | async-start | bytes 8912896 | tf_op jit(solution)/shard_map/all_gather | solution.py:18
  743.9 48.2 %copy-start.31 = (f32[12,256,64]{1,2,0:T(8,128)S(1)}, f32[12,256,64]{1,2,0:T(8,128)}, u32[]{:S(2)}) copy-start(f32[12,256,64]{1,2,0:T(8,128)} %copy-done.30) | copy-start | bytes 2359300
  743.9 465.3 %reduce-scatter.5.cloned.1.call-start = ((), (), s32[]{:S(2)}) async-start(), calls=%async_computation.10 | async-start | bytes 2506752 | tf_op jit(solution)/shard_map/reduce_scatter | solution.py:363
  802.8 18.6 %copy-start.17 = (f32[1024,768]{0,1:T(8,128)S(1)}, f32[1024,768]{0,1:T(8,128)}, u32[]{:S(2)}) copy-start(f32[1024,768]{0,1:T(8,128)} %copy-done.16) | copy-start | bytes 9437188
  802.8 18.6 %copy-start.25 = (bf16[1024,768]{0,1:T(8,128)(2,1)S(1)}, bf16[1024,768]{0,1:T(8,128)(2,1)}, u32[]{:S(2)}) copy-start(bf16[1024,768]{0,1:T(8,128)(2,1)} %fusion.49) | copy-start | bytes 4718596
  830.9 458.8 %reduce-scatter.7.cloned.1.call-start = ((), (), s32[]{:S(2)}) async-start(), calls=%async_computation.11 | async-start | bytes 7520256
  1138.1 10.8 copy-start.32
  1138.1 10.8 copy-start.35
  1138.1 10.8 copy-start.43
  1148.9 13.3 copy-start.6
  1191.7 277.3 %all-reduce.23.cloned.1.call-start = ((), (), s32[]{:S(2)}) async-start(), calls=%async_computation.12 | async-start | bytes 18874368 | tf_op jit(solution)/shard_map/psum | solution.py:357
  1209.1 68.4 %copy-start.14 = (bf16[1024,12,64]{0,2,1:T(8,128)(2,1)S(1)}, bf16[1024,12,64]{0,2,1:T(8,128)(2,1)}, u32[]{:S(2)}) copy-start(bf16[1024,12,64]{0,2,1:T(8,128)(2,1)} %fusion.48) | copy-start | bytes 4718596
  (56 other events, 300.7 us)
Sparse Core Ops, SparseCore 0:
  10.9 63.0 all-gather.15
  116.5 75.6 all-gather.17
  194.4 72.9 all-gather.19
  270.2 52.4 all-gather.21
  582.4 48.7 all-reduce.18
  654.2 51.4 all-reduce.20
  742.0 76.0 all-gather.23
  820.3 73.4 all-gather.25
  897.6 61.3 reduce-scatter.4
  1191.8 87.8 reduce-scatter.6
  1284.0 184.9 all-reduce.22
where the time goes:
time: 1500 us; the launch traced here: 1480 us
  waiting for transfers between devices  404 us (27%)
  loops' own time  378 us (25%)
  matrix products  219 us (15%)
  blocking collectives  205 us (14%)
  local copies, waits for them, and re-layouts  128 us (9%)
  other arithmetic  121 us (8%)
  between operations  26.8 us (2%)
    another operation x4, loops' own time, entering(): return lax.fori_loop(0, ahead, one, state)  378 us
    psum x1, waiting for transfers between devices, local(): lax.psum((up_weight_grad, up_bias_grad, down_weight_grad, down_bias_grad)...  178 us
    all_gather x4, waiting for transfers between devices, entering(): lax.all_gather(a.astype(kind), axis)  111 us
    unnamed x2, blocking collectives  104 us
    all_gather x5, blocking collectives, entering(): lax.all_gather(a.astype(kind), axis)  102 us
    select_n x30, other arithmetic, backward_join(): jnp.where(lower_marks[3] > 0.5, lower_moments + linked * upper_moments, u...  61.3 us
    psum x1, waiting for transfers between devices, local(): lax.psum(hidden_part.astype(jnp.bfloat16), 'mp').astype(jnp.float32)  51.6 us
    psum x1, waiting for transfers between devices, local(): lax.psum(partial_out.astype(jnp.bfloat16), 'mp').astype(jnp.float32)  46 us
  transfers between devices with their start and end apart: 11, of which 6 were waited for; matrix products, arithmetic and copies ran while one was open for 22% of the time, Pallas kernels for 0%

commit v1 on v0

v1 whole, which is shorter than its diff:
```python
from functools import partial
import math

import jax
import jax.numpy as jnp
from jax import lax
from jax.experimental import pallas as pl
from jax.experimental.pallas import tpu as pltpu
from jax.sharding import PartitionSpec as P

EPSILON = 1e-05
F32 = jnp.float32
BF16 = jnp.bfloat16
LOG2E = math.log2(math.e)
VMEM_LIMIT = 56 * 1024 * 1024
SLOTS = 8


def nn(a, b):
    return lax.dot_general(a, b, (((1,), (0,)), ((), ())), preferred_element_type=F32)


def nt(a, b):
    return lax.dot_general(a, b, (((1,), (1,)), ((), ())), preferred_element_type=F32)


def tn(a, b):
    return lax.dot_general(a, b, (((0,), (0,)), ((), ())), preferred_element_type=F32)


def fold_rows(a):
    return jnp.sum(a.reshape(a.shape[0] // 8, 8, a.shape[1]), axis=0)


def bit_pairs(count, bit):
    return [(i, i ^ bit) for i in range(count)]


def dp_bits():
    count = lax.axis_size("dp")
    bits = []
    bit = count // 2
    while bit:
        bits.append(bit)
        bit //= 2
    return bits


def swap_dp(a, bit):
    return lax.ppermute(a, "dp", bit_pairs(lax.axis_size("dp"), bit))


def swap_mp(a):
    return lax.ppermute(a, "mp", [(0, 1), (1, 0)])


def mine(bit):
    return (lax.axis_index("dp") // bit) % 2


def join_pair(own, other, bit, axis):
    low = jnp.stack([own, other], axis)
    high = jnp.stack([other, own], axis)
    return jnp.where(bit == 0, low, high)


def gather_all(a):
    bits = dp_bits()
    rank = a.ndim
    for place, bit in enumerate(bits[:-1]):
        a = join_pair(a, swap_dp(a, bit), mine(bit), place)
    place = len(bits) - 1
    a = join_pair(a, swap_mp(a), lax.axis_index("mp"), place)
    a = join_pair(a, swap_dp(a, 1), mine(1), place)
    return a.reshape((-1,) + a.shape[a.ndim - rank + 1 :])


def scatter_sum(a):
    bits = dp_bits()
    count = lax.axis_size("dp")
    a = a.reshape((2,) * len(bits) + (a.shape[0] // count,) + a.shape[1:])
    left = list(bits)
    for bit in reversed(bits):
        axis = left.index(bit)
        left.pop(axis)
        own = lax.dynamic_index_in_dim(a, mine(bit), axis, False)
        send = lax.dynamic_index_in_dim(a, 1 - mine(bit), axis, False)
        got = swap_dp(send, bit)
        a = (own.astype(F32) + got.astype(F32)).astype(a.dtype)
    return a


def gather_dp(a):
    bits = dp_bits()
    for place, bit in enumerate(bits):
        a = join_pair(a, swap_dp(a, bit), mine(bit), place)
    return a.reshape((-1,) + a.shape[len(bits) + 1 :])


def sum_dp(a):
    return gather_dp(scatter_sum(a))


def other_half(a):
    rows = a.shape[0] // 2
    core = mine(1)
    part = lax.dynamic_slice_in_dim(a, core * rows, rows, 0)
    part = swap_mp(part)
    whole = join_pair(part, swap_dp(part, 1), core, 0)
    return whole.reshape(a.shape)


def full(shape):
    return pl.BlockSpec(shape, lambda t, *_: (0,) * len(shape), pipeline_mode=pl.Buffered(1))


def rows(tile, width):
    return pl.BlockSpec((tile, width), lambda t, *_: (t, 0))


def held(shape):
    return pl.BlockSpec(shape, lambda t, *_: (0,) * len(shape))


def call(kernel, tiles, in_specs, outs, scratch, flops):
    return pl.pallas_call(
        kernel,
        grid_spec=pltpu.PrefetchScalarGridSpec(
            num_scalar_prefetch=1,
            grid=(tiles,),
            in_specs=in_specs,
            out_specs=[spec for spec, _, _ in outs],
            scratch_shapes=scratch,
        ),
        out_shape=[jax.ShapeDtypeStruct(shape, kind) for _, shape, kind in outs],
        compiler_params=pltpu.CompilerParams(
            vmem_limit_bytes=VMEM_LIMIT, dimension_semantics=("arbitrary",)
        ),
        cost_estimate=pl.CostEstimate(flops=int(flops), bytes_accessed=20_000_000, transcendentals=0),
    )


def features(scaled, table):
    lhs = jnp.concatenate([scaled.astype(BF16), (-0.5 * scaled * scaled).astype(BF16)], axis=1)
    return jnp.exp2(nn(lhs, table) * LOG2E - 4.0)


def pack_tables(source, base, mass_base, table, masses, acc, macc):
    pairs = acc.shape[0]
    for p in range(pairs):
        for k in range(2):
            head = 2 * p + k
            table[pl.ds(base + head * 64, 64), :] = acc[
                p, k * 64 : (k + 1) * 64, k * 256 : (k + 1) * 256
            ].astype(table.dtype)
            masses[pl.ds(mass_base + head, 1), :] = jnp.sum(
                macc[p, :, k * 256 : (k + 1) * 256], axis=0, keepdims=True
            )


def unpack_tables(tabs, slot, table, base, masses, mass_base, repeat):
    pairs = tabs.shape[1]
    for p in range(pairs):
        for k in range(2):
            head = 2 * p + k
            span = slice(k * 256, (k + 1) * 256)
            tabs[slot, p, k * 64 : (k + 1) * 64, span] = table[pl.ds(base + head * 64, 64), :]
            mass = masses[pl.ds(mass_base + head, 1), :]
            if repeat:
                tabs[slot, p, 128 + k * 64 : 192 + k * 64, span] = jnp.broadcast_to(
                    mass, (64, 256)
                ).astype(BF16)
            else:
                high = mass.astype(BF16).astype(F32)
                index = lax.broadcasted_iota(jnp.int32, (64, 256), 0)
                spread = jnp.where(
                    index == 0,
                    jnp.broadcast_to(high, (64, 256)),
                    jnp.where(index == 1, jnp.broadcast_to(mass - high, (64, 256)), 0.0),
                )
                tabs[slot, p, 128 + k * 64 : 192 + k * 64, span] = spread.astype(BF16)


def fill_tables(flags, tabs, main, main_masses, small, small_masses, repeat):
    heads_rows = main.shape[0]
    mass_rows = main_masses.shape[0]
    tabs[...] = jnp.zeros_like(tabs)
    unpack_tables(tabs, 0, main, 0, main_masses, 0, repeat)

    @pl.when(flags[0, 9] > 0)
    def _():
        for j in range(1, SLOTS):
            unpack_tables(
                tabs, j, small, (j - 1) * heads_rows, small_masses, (j - 1) * mass_rows, repeat
            )


def keys_kernel(
    flags, x, weight, bias, table, slot,
    phi, values, scaled_out, main, main_masses, small, small_masses,
    acc, macc, sacc, smacc,
):
    t = pl.program_id(0)
    pairs = table.shape[0]
    width = pairs * 128
    slow_any = flags[0, 9] > 0

    @pl.when(t == 0)
    def _():
        acc[...] = jnp.zeros_like(acc)
        macc[...] = jnp.zeros_like(macc)

        @pl.when(slow_any)
        def _():
            sacc[...] = jnp.zeros_like(sacc)
            smacc[...] = jnp.zeros_like(smacc)

    both = nn(x[...], weight[...]) + bias[...]
    values[...] = both[:, width:].astype(BF16)
    for p in range(pairs):
        scaled = both[:, p * 128 : (p + 1) * 128] * 64 ** (-0.25)
        scaled_out[:, p * 128 : (p + 1) * 128] = scaled.astype(BF16)
        phi[:, p * 512 : (p + 1) * 512] = features(scaled, table[p]).astype(BF16)

    @pl.when(flags[t, 0] > 0)
    def _():
        for p in range(pairs):
            part = phi[:, p * 512 : (p + 1) * 512]
            acc[p] += tn(values[:, p * 128 : (p + 1) * 128], part)
            macc[p] += fold_rows(part.astype(F32))

    @pl.when(flags[t, 0] == 0)
    def _():
        def one(j, carry):
            @pl.when(flags[t, 1 + j] > 0)
            def _():
                mask = slot[...] == j
                wide = jnp.concatenate([mask] * 4, axis=1)
                for p in range(pairs):
                    part = phi[:, p * 512 : (p + 1) * 512]
                    value = values[:, p * 128 : (p + 1) * 128].astype(F32)
                    moment = tn(jnp.where(mask, value, 0.0).astype(BF16), part)
                    mass = fold_rows(jnp.where(wide, part.astype(F32), 0.0))

                    @pl.when(j == 0)
                    def _():
                        acc[p] += moment
                        macc[p] += mass

                    @pl.when(j > 0)
                    def _():
                        sacc[j - 1, p] += moment
                        smacc[j - 1, p] += mass

            return carry

        lax.fori_loop(0, SLOTS, one, 0)

    @pl.when(t == pl.num_programs(0) - 1)
    def _():
        pack_tables(None, 0, 0, main, main_masses, acc, macc)

        @pl.when(slow_any)
        def _():
            for j in range(SLOTS - 1):
                pack_tables(
                    None, j * main.shape[0], j * main_masses.shape[0], small, small_masses,
                    sacc.at[j], smacc.at[j],
                )


def queries_kernel(flags, x, weight, bias, table, select, phi, scaled_out, chosen):
    pairs = table.shape[0]
    query = nn(x[...], weight[...]) + bias[...]
    chosen[...] = nn(x[...], select[...]).astype(BF16)
    for p in range(pairs):
        scaled = query[:, p * 128 : (p + 1) * 128] * 64 ** (-0.25)
        scaled_out[:, p * 128 : (p + 1) * 128] = scaled.astype(BF16)
        phi[:, p * 512 : (p + 1) * 512] = features(scaled, table[p]).astype(BF16)


def center(z):
    average = jnp.mean(z, axis=1, keepdims=True)
    centered = z - average
    inverse = lax.rsqrt(jnp.mean(centered * centered, axis=1, keepdims=True) + EPSILON)
    return centered * inverse, inverse


def center_back(e, normed, inverse):
    first = jnp.mean(e, axis=1, keepdims=True)
    second = jnp.mean(e * normed, axis=1, keepdims=True)
    return inverse * (e - first - normed * second)


def middle_kernel(
    flags, x, cot, slot, phi, main, main_masses, small, small_masses,
    out_weight, up_own, up_other, down_own, down_other, bias_own, bias_other, vectors,
    layer_out, hidden_grad, normed_out, inverse_out, att_out, invden_out,
    active_out, dup_out, hidden_out, dffn_out, sums, up_sum,
    tabs, spread, gates,
):
    t = pl.program_id(0)
    pairs = tabs.shape[1]
    width = pairs * 128

    @pl.when(t == 0)
    def _():
        fill_tables(flags, tabs, main, main_masses, small, small_masses, True)
        sums[...] = jnp.zeros_like(sums)
        up_sum[...] = jnp.zeros_like(up_sum)

    @pl.when(flags[t, 0] > 0)
    def _():
        for p in range(pairs):
            spread[:, p * 256 : (p + 1) * 256] = nt(phi[:, p * 512 : (p + 1) * 512], tabs[0, p])

    @pl.when(flags[t, 0] == 0)
    def _():
        spread[...] = jnp.zeros_like(spread)

        def one(j, carry):
            @pl.when(flags[t, 1 + j] > 0)
            def _():
                mask = slot[...] == j
                wide = jnp.concatenate([mask] * 2, axis=1)
                for p in range(pairs):
                    got = nt(phi[:, p * 512 : (p + 1) * 512], tabs[j, p])
                    old = spread[:, p * 256 : (p + 1) * 256]
                    spread[:, p * 256 : (p + 1) * 256] = jnp.where(wide, got, old)

            return carry

        lax.fori_loop(0, SLOTS, one, 0)

    live = slot[...] < SLOTS
    for p in range(pairs):
        numerator = spread[:, p * 256 : p * 256 + 128]
        denominator = spread[:, p * 256 + 128 : (p + 1) * 256]
        inverse = jnp.where(live, 1.0 / jnp.where(live, denominator, 1.0), 0.0)
        invden_out[:, p * 128 : (p + 1) * 128] = inverse
        att_out[:, p * 128 : (p + 1) * 128] = (numerator * inverse).astype(BF16)

    def vector(i):
        return vectors[i : i + 1, :]

    branch = nn(att_out[...], out_weight[...]) + vector(0)
    first, first_inverse = center(x[...].astype(F32) + branch)
    normed_out[...] = first
    inverse_out[...] = jnp.broadcast_to(first_inverse, inverse_out.shape)
    hidden = first * vector(1) + vector(2)
    hidden_low = hidden.astype(BF16)
    hidden_out[...] = hidden_low
    step = 512
    half = up_own.shape[1]
    chunks = [(up_own, down_own, bias_own, 0, c, c) for c in range(0, half, step)]
    chunks += [(up_other, down_other, bias_other, 1, c, half + c) for c in range(0, half, step)]
    total = hidden + vector(3)
    other_active = []
    for up, down, bias, which, c, place in chunks:
        value = nn(hidden_low, up[:, c : c + step]) + bias[:, c : c + step]
        cdf = 0.5 + 0.5 * lax.erf(value * math.sqrt(0.5))
        gates[:, place : place + step] = cdf + value * jnp.exp2(
            value * value * (-0.5 * LOG2E)
        ) * (1.0 / math.sqrt(2.0 * math.pi))
        active = (value * cdf).astype(BF16)
        if which == 0:
            active_out[:, c : c + step] = active
        total = total + nn(active, down[c : c + step, :])
    second, second_inverse = center(total)
    layer_out[...] = (second * vector(4) + vector(5)).astype(BF16)
    g = cot[...].astype(F32)
    sums[0:8, :] += fold_rows(g * second)
    sums[8:16, :] += fold_rows(g)
    dsecond = center_back(g * vector(4), second, second_inverse)
    dffn = dsecond.astype(BF16)
    dffn_out[...] = dffn
    sums[16:24, :] += fold_rows(dffn.astype(F32))
    for up, down, bias, which, c, place in chunks:
        dup = (nt(dffn, down[c : c + step, :]) * gates[:, place : place + step]).astype(BF16)
        if which == 0:
            dup_out[:, c : c + step] = dup
            up_sum[:, c : c + step] += fold_rows(dup.astype(F32))
        dsecond = dsecond + nt(dup, up[:, c : c + step])
    hidden_grad[...] = dsecond


def attention_back_kernel(
    flags, hidden_grad, normed, inverse, att, invden, phi, slot, out_weight, gain, select,
    dfirst_out, dbranch_out, mixed, chosen, sums, main, main_masses, small, small_masses,
    acc, sacc,
):
    t = pl.program_id(0)
    pairs = acc.shape[0]
    slow_any = flags[0, 9] > 0

    @pl.when(t == 0)
    def _():
        acc[...] = jnp.zeros_like(acc)
        sums[...] = jnp.zeros_like(sums)

        @pl.when(slow_any)
        def _():
            sacc[...] = jnp.zeros_like(sacc)

    grad = hidden_grad[...]
    first = normed[...]
    sums[0:8, :] += fold_rows(grad * first)
    sums[8:16, :] += fold_rows(grad)
    dfirst = center_back(grad * gain[...], first, inverse[:, 0:1])
    dfirst_out[...] = dfirst
    dbranch = dfirst.astype(BF16)
    dbranch_out[...] = dbranch
    sums[16:24, :] += fold_rows(dbranch.astype(F32))
    chosen[...] = nn(att[...], select[...]).astype(BF16)
    datt = nt(dbranch, out_weight[...])
    ratio = datt * invden[...]
    dden = -ratio * att[...].astype(F32)
    for p in range(pairs):
        mixed[:, p * 256 : p * 256 + 128] = ratio[:, p * 128 : (p + 1) * 128].astype(BF16)
        mixed[:, p * 256 + 128 : (p + 1) * 256] = dden[:, p * 128 : (p + 1) * 128].astype(BF16)

    @pl.when(flags[t, 0] > 0)
    def _():
        for p in range(pairs):
            acc[p] += tn(mixed[:, p * 256 : (p + 1) * 256], phi[:, p * 512 : (p + 1) * 512])

    @pl.when(flags[t, 0] == 0)
    def _():
        def one(j, carry):
            @pl.when(flags[t, 1 + j] > 0)
            def _():
                mask = slot[...] == j
                wide = jnp.concatenate([mask] * 2, axis=1)
                for p in range(pairs):
                    part = mixed[:, p * 256 : (p + 1) * 256].astype(F32)
                    moment = tn(
                        jnp.where(wide, part, 0.0).astype(BF16), phi[:, p * 512 : (p + 1) * 512]
                    )

                    @pl.when(j == 0)
                    def _():
                        acc[p] += moment

                    @pl.when(j > 0)
                    def _():
                        sacc[j - 1, p] += moment

            return carry

        lax.fori_loop(0, SLOTS, one, 0)

    def pack(table, base, masses, mass_base, source):
        for p in range(pairs):
            for k in range(2):
                head = 2 * p + k
                span = slice(k * 256, (k + 1) * 256)
                table[pl.ds(base + head * 64, 64), :] = source[
                    p, k * 64 : (k + 1) * 64, span
                ].astype(BF16)
                masses[pl.ds(mass_base + head, 1), :] = jnp.sum(
                    source[p, 128 + k * 64 : 192 + k * 64, span], axis=0, keepdims=True
                )

    @pl.when(t == pl.num_programs(0) - 1)
    def _():
        pack(main, 0, main_masses, 0, acc)

        @pl.when(slow_any)
        def _():
            for j in range(SLOTS - 1):
                pack(small, j * main.shape[0], small_masses, j * main_masses.shape[0], sacc.at[j])


def masked_product(flags, t, slot, left, tabs, p, result):
    result[...] = jnp.zeros_like(result)

    def one(j, carry):
        @pl.when(flags[t, 1 + j] > 0)
        def _():
            mask = slot[...] == j
            wide = jnp.concatenate([mask] * 2, axis=1)
            part = jnp.where(wide, left.astype(F32), 0.0).astype(BF16)
            result[...] += nn(part, tabs[j, p])

        return carry

    lax.fori_loop(0, SLOTS, one, 0)


def queries_back_kernel(
    flags, mixed, phi, scaled, slot, main, main_masses, small, small_masses, table, weight, dfirst,
    dquery_out, partial_out, sums, tabs, work,
):
    t = pl.program_id(0)
    pairs = tabs.shape[1]

    @pl.when(t == 0)
    def _():
        fill_tables(flags, tabs, main, main_masses, small, small_masses, True)
        sums[...] = jnp.zeros_like(sums)

    def finish(p, grad):
        span = slice(p * 128, (p + 1) * 128)
        e = (grad * phi[:, p * 512 : (p + 1) * 512].astype(F32)).astype(BF16)
        back = nt(e, table[p])
        du = (back[:, :128] - scaled[:, span].astype(F32) * back[:, 128:]) * 64 ** (-0.25)
        dquery_out[:, span] = du.astype(BF16)

    @pl.when(flags[t, 0] > 0)
    def _():
        for p in range(pairs):
            finish(p, nn(mixed[:, p * 256 : (p + 1) * 256], tabs[0, p]))

    @pl.when(flags[t, 0] == 0)
    def _():
        for p in range(pairs):
            masked_product(flags, t, slot, mixed[:, p * 256 : (p + 1) * 256], tabs, p, work)
            finish(p, work[...])

    sums[...] += fold_rows(dquery_out[...].astype(F32))
    partial_out[...] = dfirst[...] + nt(dquery_out[...], weight[...])


def keys_back_kernel(
    flags, phi, values, scaled, slot, main, main_masses, small, small_masses, table, weight, partial_in,
    djoint_out, tokens_out, sums, tabs, work, vwork,
):
    t = pl.program_id(0)
    pairs = tabs.shape[1]
    width = pairs * 128

    @pl.when(t == 0)
    def _():
        fill_tables(flags, tabs, main, main_masses, small, small_masses, False)
        sums[...] = jnp.zeros_like(sums)

    def extended(p):
        value = values[:, p * 128 : (p + 1) * 128]
        return jnp.concatenate([value, jnp.ones_like(value)], axis=1)

    def finish(p, grad):
        span = slice(p * 128, (p + 1) * 128)
        e = (grad * phi[:, p * 512 : (p + 1) * 512].astype(F32)).astype(BF16)
        back = nt(e, table[p])
        du = (back[:, :128] - scaled[:, span].astype(F32) * back[:, 128:]) * 64 ** (-0.25)
        djoint_out[:, span] = du.astype(BF16)

    @pl.when(flags[t, 0] > 0)
    def _():
        for p in range(pairs):
            finish(p, nn(extended(p), tabs[0, p]))
            dvalue = nt(phi[:, p * 512 : (p + 1) * 512], tabs[0, p, :128, :])
            djoint_out[:, width + p * 128 : width + (p + 1) * 128] = dvalue.astype(BF16)

    @pl.when(flags[t, 0] == 0)
    def _():
        for p in range(pairs):
            masked_product(flags, t, slot, extended(p), tabs, p, work)
            finish(p, work[...])
            vwork[...] = jnp.zeros_like(vwork)

            def one(j, carry):
                @pl.when(flags[t, 1 + j] > 0)
                def _():
                    got = nt(phi[:, p * 512 : (p + 1) * 512], tabs[j, p, :128, :])
                    vwork[...] = jnp.where(slot[...] == j, got, vwork[...])

                return carry

            lax.fori_loop(0, SLOTS, one, 0)
            djoint_out[:, width + p * 128 : width + (p + 1) * 128] = vwork[...].astype(BF16)

    sums[...] += fold_rows(djoint_out[...].astype(F32))
    tokens_out[...] = (partial_in[...] + nt(djoint_out[...], weight[...])).astype(BF16)


def local(
    tokens, document_lengths, feature_maps, joint_weight, joint_bias, output_weight, output_bias,
    first_gain, first_shift, up_weight, up_bias, down_weight, down_bias, second_gain, second_shift,
    cotangent,
):
    count, width = tokens.shape
    heads, head_size, feature_count = feature_maps.shape
    pairs = heads // 2
    half = up_weight.shape[1]
    tile = 256
    tiles = count // tile
    rank = lax.axis_index("dp")
    dp = lax.axis_size("dp")
    mp = lax.axis_size("mp")
    mp_rank = lax.axis_index("mp")

    lengths = document_lengths[0]
    ends = jnp.cumsum(lengths)
    place = rank * count + jnp.arange(count, dtype=jnp.int32)
    document = jnp.sum((ends[None, :] <= place[:, None]).astype(jnp.int32), axis=1)
    longest = jnp.argmax(lengths).astype(jnp.int32)
    slot = jnp.where(
        document == longest,
        0,
        jnp.where(document >= SLOTS, SLOTS, jnp.where(document < longest, document + 1, document)),
    )
    slots = jnp.broadcast_to(slot[:, None], (count, 128))
    present = jnp.max(
        (slot.reshape(tiles, tile)[:, :, None] == jnp.arange(SLOTS)[None, None, :]).astype(jnp.int32),
        axis=1,
    )
    all_main = jnp.max(slot.reshape(tiles, tile), axis=1, keepdims=True) == 0
    any_slow = jnp.broadcast_to(jnp.max(slot) > 0, (tiles, 1))
    flags = jnp.concatenate(
        [all_main.astype(jnp.int32), present, any_slow.astype(jnp.int32), jnp.zeros((tiles, 6), jnp.int32)],
        axis=1,
    )

    shard = joint_weight.shape[0]
    small_vectors = jnp.concatenate(
        [joint_bias, output_bias, first_gain, first_shift, second_gain, second_shift]
    )
    small_vectors = jnp.pad(small_vectors, (0, 256 - small_vectors.shape[0]))[None, :]
    vectors_all = gather_all(small_vectors)
    key_value = gather_all(joint_weight[:, width:])
    query_out = gather_all(jnp.concatenate([joint_weight[:, :width], output_weight], axis=1))
    query_weight = query_out[:, :width]
    out_weight = query_out[:, width:]
    bias_part = joint_bias.shape[0]
    joint_offset = vectors_all[:, :bias_part].reshape(1, -1).astype(F32)
    parts = [
        vectors_all[:, bias_part + i * shard : bias_part + (i + 1) * shard].reshape(-1).astype(F32)
        for i in range(5)
    ]
    vectors = jnp.stack(
        [parts[0], parts[1], parts[2], down_bias.astype(F32), parts[3], parts[4], parts[4], parts[4]]
    )
    up_other = other_half(up_weight)
    down_other = other_half(down_weight)
    bias_own = up_bias[None, :].astype(F32)
    bias_other = swap_mp(up_bias[None, :]).astype(F32)

    pair_maps = feature_maps.reshape(pairs, 2, head_size, feature_count)
    blank = jnp.zeros_like(pair_maps[:, 0])
    table = jnp.concatenate(
        [
            jnp.concatenate([pair_maps[:, 0], blank], axis=2),
            jnp.concatenate([blank, pair_maps[:, 1]], axis=2),
            jnp.concatenate([blank + 1, blank], axis=2),
            jnp.concatenate([blank, blank + 1], axis=2),
        ],
        axis=1,
    )
    own_rows = width // mp
    index = jnp.arange(own_rows, dtype=jnp.int32)
    source = index // shard * (shard * mp) + mp_rank * shard + index % shard
    select = (jnp.arange(width, dtype=jnp.int32)[:, None] == source[None, :]).astype(BF16)

    mass_rows = 16
    wide = pairs * 512
    table_spec = full((pairs, 256, 512))
    sm_rows = (SLOTS - 1) * width
    sm_mass = (SLOTS - 1) * mass_rows

    phi_k, values, scaled_k, moments, masses, small_moments, small_masses = call(
        keys_kernel,
        tiles,
        [rows(tile, width), full((width, 2 * width)), full((1, 2 * width)), table_spec, rows(tile, 128)],
        [
            (rows(tile, wide), (count, wide), BF16),
            (rows(tile, width), (count, width), BF16),
            (rows(tile, width), (count, width), BF16),
            (held((width, 256)), (width, 256), BF16),
            (held((mass_rows, 256)), (mass_rows, 256), F32),
            (held((sm_rows, 256)), (sm_rows, 256), BF16),
            (held((sm_mass, 256)), (sm_mass, 256), F32),
        ],
        [
            pltpu.VMEM((pairs, 128, 512), F32),
            pltpu.VMEM((pairs, 8, 512), F32),
            pltpu.VMEM((SLOTS - 1, pairs, 128, 512), F32),
            pltpu.VMEM((SLOTS - 1, pairs, 8, 512), F32),
        ],
        10e9,
    )(flags, tokens, key_value, joint_offset[:, width:], table, slots)

    def sum_tables(main, main_masses):
        pad = -(width + mass_rows) % (8 * dp)
        packed = jnp.concatenate(
            [main, main_masses.astype(BF16), jnp.zeros((pad, 256), BF16)], axis=0
        )
        packed = sum_dp(packed)
        return packed[:width], packed[width : width + mass_rows].astype(F32)

    moments, masses = sum_tables(moments, masses)

    phi_q, scaled_q, tokens_own = call(
        queries_kernel,
        tiles,
        [rows(tile, width), full((width, width)), full((1, width)), table_spec, full((width, own_rows))],
        [
            (rows(tile, wide), (count, wide), BF16),
            (rows(tile, width), (count, width), BF16),
            (rows(tile, own_rows), (count, own_rows), BF16),
        ],
        [],
        6e9,
    )(flags, tokens, query_weight, joint_offset[:, :width], table, select)

    moment_specs = [
        full((width, 256)),
        full((mass_rows, 256)),
        full((sm_rows, 256)),
        full((sm_mass, 256)),
    ]
    (
        layer_output, hidden_grad, normed, inverse, att, invden, active, dup, hidden_low, dffn, sums, up_sum,
    ) = call(
        middle_kernel,
        tiles,
        [rows(tile, width), rows(tile, width), rows(tile, 128), rows(tile, wide)]
        + moment_specs
        + [
            full((width, width)),
            full((width, half)),
            full((width, half)),
            full((half, width)),
            full((half, width)),
            full((1, half)),
            full((1, half)),
            full((8, width)),
        ],
        [
            (rows(tile, width), (count, width), BF16),
            (rows(tile, width), (count, width), F32),
            (rows(tile, width), (count, width), F32),
            (rows(tile, 128), (count, 128), F32),
            (rows(tile, width), (count, width), BF16),
            (rows(tile, width), (count, width), F32),
            (rows(tile, half), (count, half), BF16),
            (rows(tile, half), (count, half), BF16),
            (rows(tile, width), (count, width), BF16),
            (rows(tile, width), (count, width), BF16),
            (held((24, width)), (24, width), F32),
            (held((8, half)), (8, half), F32),
        ],
        [
            pltpu.VMEM((SLOTS, pairs, 256, 512), BF16),
            pltpu.VMEM((tile, pairs * 256), F32),
            pltpu.VMEM((tile, 2 * half), F32),
        ],
        30e9,
    )(
        flags, tokens, cotangent, slots, phi_q, moments, masses, small_moments, small_masses,
        out_weight, up_weight, up_other, down_weight, down_other, bias_own, bias_other, vectors,
    )

    down_grad = tn(active, dffn).astype(BF16)
    up_grad = tn(hidden_low, dup).astype(BF16)

    dfirst, dbranch, mixed, att_own, first_sums, dmoments, dmasses, small_dmoments, small_dmasses = call(
        attention_back_kernel,
        tiles,
        [
            rows(tile, width), rows(tile, width), rows(tile, 128), rows(tile, width), rows(tile, width),
            rows(tile, wide), rows(tile, 128), full((width, width)), full((1, width)), full((width, own_rows)),
        ],
        [
            (rows(tile, width), (count, width), F32),
            (rows(tile, width), (count, width), BF16),
            (rows(tile, 2 * width), (count, 2 * width), BF16),
            (rows(tile, own_rows), (count, own_rows), BF16),
            (held((24, width)), (24, width), F32),
            (held((width, 256)), (width, 256), BF16),
            (held((mass_rows, 256)), (mass_rows, 256), F32),
            (held((sm_rows, 256)), (sm_rows, 256), BF16),
            (held((sm_mass, 256)), (sm_mass, 256), F32),
        ],
        [
            pltpu.VMEM((pairs, 256, 512), F32),
            pltpu.VMEM((SLOTS - 1, pairs, 256, 512), F32),
        ],
        6e9,
    )(flags, hidden_grad, normed, inverse, att, invden, phi_q, slots, out_weight, vectors[1:2], select)

    dmoments, dmasses = sum_tables(dmoments, dmasses)

    dquery, partial_tokens, query_sums = call(
        queries_back_kernel,
        tiles,
        [rows(tile, 2 * width), rows(tile, wide), rows(tile, width), rows(tile, 128)]
        + moment_specs
        + [table_spec, full((width, width)), rows(tile, width)],
        [
            (rows(tile, width), (count, width), BF16),
            (rows(tile, width), (count, width), F32),
            (held((8, width)), (8, width), F32),
        ],
        [pltpu.VMEM((SLOTS, pairs, 256, 512), BF16), pltpu.VMEM((tile, 512), F32)],
        8e9,
    )(
        flags, mixed, phi_q, scaled_q, slots, moments, masses, small_moments, small_masses, table,
        query_weight, dfirst,
    )

    out_grad = tn(att_own, dbranch).astype(BF16)
    query_grad = tn(tokens_own, dquery).astype(BF16)

    dkey_value, tokens_grad, key_sums = call(
        keys_back_kernel,
        tiles,
        [rows(tile, wide), rows(tile, width), rows(tile, width), rows(tile, 128)]
        + moment_specs
        + [table_spec, full((width, 2 * width)), rows(tile, width)],
        [
            (rows(tile, 2 * width), (count, 2 * width), BF16),
            (rows(tile, width), (count, width), BF16),
            (held((8, 2 * width)), (8, 2 * width), F32),
        ],
        [
            pltpu.VMEM((SLOTS, pairs, 256, 512), BF16),
            pltpu.VMEM((tile, 512), F32),
            pltpu.VMEM((tile, 128), F32),
        ],
        12e9,
    )(
        flags, phi_k, values, scaled_k, slots, dmoments, dmasses, small_dmoments, small_dmasses, table,
        key_value, partial_tokens,
    )
    key_value_grad = tn(tokens_own, dkey_value).astype(BF16)

    down_total = sum_dp(down_grad)
    up_total = sum_dp(up_grad)
    small_sums = jnp.concatenate(
        [
            jnp.sum(query_sums, axis=0),
            jnp.sum(key_sums, axis=0),
            jnp.sum(first_sums.reshape(3, 8, width), axis=1).reshape(-1),
            jnp.sum(sums.reshape(3, 8, width), axis=1).reshape(-1),
            jnp.sum(up_sum, axis=0),
        ]
    )
    pad = -small_sums.shape[0] % (dp * 8 * 128)
    small_sums = sum_dp(jnp.pad(small_sums, (0, pad)).reshape(-1, 128)).reshape(-1)
    attention_total = scatter_sum(
        jnp.concatenate([query_grad, key_value_grad, out_grad], axis=1)
    ).astype(F32)

    def owned(start, size):
        part = size // (dp * mp)
        return lax.dynamic_slice_in_dim(small_sums, start + (rank * mp + mp_rank) * part, part, 0)

    return (
        layer_output,
        tokens_grad,
        attention_total[:, : 3 * width],
        owned(0, 3 * width),
        attention_total[:, 3 * width :],
        owned(5 * width, width),
        owned(3 * width, width),
        owned(4 * width, width),
        up_total.astype(F32),
        small_sums[9 * width : 9 * width + half],
        down_total.astype(F32),
        small_sums[8 * width : 9 * width],
        owned(6 * width, width),
        owned(7 * width, width),
    )


def solution(mesh):
    shared = P(("dp", "mp"))
    in_specs = (
        P("dp", None), P(), P(), P(("dp", "mp"), None), shared, P(("dp", "mp"), None), shared, shared,
        shared, P(None, "mp"), P("mp"), P("mp", None), P(), shared, shared, P("dp", None),
    )
    out_specs = (
        P("dp", None), P("dp", None), P(("dp", "mp"), None), shared, P(("dp", "mp"), None), shared,
        shared, shared, P(None, "mp"), P("mp"), P("mp", None), P(), shared, shared,
    )
    return jax.shard_map(local, mesh=mesh, in_specs=in_specs, out_specs=out_specs, check_vma=False)
```

time: 1500 us -> 529 us (0.35)
  loops' own time: 378 us -> 0 us
  waiting for transfers between devices: 404 us -> 177 us
  blocking collectives: 205 us -> 0 us
  matrix products: 219 us -> 14.7 us
  Pallas kernels: 0 us -> 136 us
  starting transfers between devices: 0.74 us -> 94.9 us
  local copies, waits for them, and re-layouts: 128 us -> 49.6 us
  other arithmetic: 121 us -> 45.5 us
  between operations: 26.8 us -> 3.08 us
    another operation x4 -> x0, loops' own time: 378 us -> none  [entering(): return lax.fori_loop(0, ahead, one, state)]
    psum x3 -> x0, waiting for transfers between devices: 275 us -> none  [the longest x1 178 us: local(): lax.psum((up_weight_grad, up_bias_grad, down_weight_grad, down_bias_grad)...]
    dot_general x26 -> x5, matrix products: 206 us -> 14.7 us  [tn(): lax.dot_general(a, b, (((0,), (0,)), ((), ())), preferred_element_type=F32)]
    ppermute x0 -> x64, waiting for transfers between devices: none -> 177 us  [the longest x58 127 us: swap_dp(): return lax.ppermute(a, 'dp', bit_pairs(lax.axis_size('dp'), bit))]
    pallas_call x0 -> x6, Pallas kernels: none -> 136 us  [the longest x1 45.5 us: local(): call(middle_kernel, tiles, [rows(tile, width), rows(tile, width), rows(ti...]
    all_gather x6 -> x0, waiting for transfers between devices: 128 us -> none  [the longest x4 111 us: entering(): lax.all_gather(a.astype(kind), axis)]
    unnamed x2 -> x0, blocking collectives: 104 us -> none
    all_gather x5 -> x0, blocking collectives: 102 us -> none  [entering(): lax.all_gather(a.astype(kind), axis)]
  transfers between devices with their start and end apart: 11 -> 64, of which waited for: 6 -> 36; matrix products, arithmetic and copies ran while one was open for 22% -> 18% of each run, Pallas kernels for 0% -> 17%
where the time goes in v1:
time: 529 us; the launch traced here: 521 us
  waiting for transfers between devices  177 us (33%)
  Pallas kernels  136 us (26%)
  starting transfers between devices  94.9 us (18%)
  local copies, waits for them, and re-layouts  49.6 us (9%)
  other arithmetic  45.5 us (9%)
  matrix products  14.7 us (3%)
    ppermute x58, waiting for transfers between devices, swap_dp(): return lax.ppermute(a, 'dp', bit_pairs(lax.axis_size('dp'), bit))  127 us
    ppermute x58, starting transfers between devices, swap_dp(): return lax.ppermute(a, 'dp', bit_pairs(lax.axis_size('dp'), bit))  89.5 us
    ppermute x6, waiting for transfers between devices, swap_mp(): return lax.ppermute(a, 'mp', [(0, 1), (1, 0)])  50.3 us
    pallas_call x1, Pallas kernels, local(): call(middle_kernel, tiles, [rows(tile, width), rows(tile, width), rows(ti...  45.5 us
    pallas_call x1, Pallas kernels, local(): call(keys_back_kernel, tiles, [rows(tile, wide), rows(tile, width), rows(...  24.9 us
    pallas_call x1, Pallas kernels, local(): call(attention_back_kernel, tiles, [rows(tile, width), rows(tile, width),...  20.7 us
    pallas_call x1, Pallas kernels, local(): call(queries_back_kernel, tiles, [rows(tile, 2 * width), rows(tile, wide)...  18.9 us
    pallas_call x1, Pallas kernels, local(): call(keys_kernel, tiles, [rows(tile, width), full((width, 2 * width)), fu...  16.9 us
  transfers between devices with their start and end apart: 64, of which 36 were waited for; matrix products, arithmetic and copies ran while one was open for 18% of the time, Pallas kernels for 17%

profile of v1, /device:TPU:0, one launch (start us, length us, event | category | flops | bytes accessed | tf_op | source)
XLA Modules:
  0.0 520.7 jit_solution(16811881942887496727)
XLA Ops:
  0.6 4.1 concatenate.828
  4.8 4.1 collective-permute-start.5
  39.8 31.5 %collective-permute-done.8 = bf16[2,2,2,1,256]{4,1,0,3,2:T(2,128)(2,1)S(1)} collective-permute-done((bf16[2,2,2,1,256]{4,1,0,3,2:T(2,128)(2,1)S(1)}, bf16[2,2,2,1,256]{4,1,0,3,2:T(2,128)(2,1)S(1)}, u32[]{:S(2)}, u32[]{:S(2)}) %collective-permute-start.8) | collective-permute-done | bytes 4128 | tf_op jit(solution)/shard_map/ppermute | solution.py:54
  91.4 3.9 collective-permute-done.11
  97.8 7.7 %collective-permute-done.12 = bf16[2,2,24,1536]{3,2,0,1:T(8,128)(2,1)S(1)} collective-permute-done((bf16[2,2,24,1536]{3,2,0,1:T(8,128)(2,1)S(1)}, bf16[2,2,24,1536]{3,2,0,1:T(8,128)(2,1)S(1)}, u32[]{:S(2)}, u32[]{:S(2)}) %collective-permute-start.12) | collective-permute-done | bytes 294944 | tf_op jit(solution)/shard_map/ppermute | solution.py:50
  106.1 4.0 collective-permute-done.2
  111.0 10.8 %collective-permute-done.13 = bf16[2,2,2,24,1536]{4,3,0,1,2:T(8,128)(2,1)S(1)} collective-permute-done((bf16[2,2,2,24,1536]{4,3,0,1,2:T(8,128)(2,1)S(1)}, bf16[2,2,2,24,1536]{4,3,0,1,2:T(8,128)(2,1)S(1)}, u32[]{:S(2)}, u32[]{:S(2)}) %collective-permute-start.13) | collective-permute-done | bytes 589856 | tf_op jit(solution)/shard_map/ppermute | solution.py:54
  122.3 8.0 %collective-permute-done.3 = bf16[2,2,2,24,1536]{4,3,0,1,2:T(8,128)(2,1)S(1)} collective-permute-done((bf16[2,2,2,24,1536]{4,3,0,1,2:T(8,128)(2,1)S(1)}, bf16[2,2,2,24,1536]{4,3,0,1,2:T(8,128)(2,1)S(1)}, u32[]{:S(2)}, u32[]{:S(2)}) %collective-permute-start.3) | collective-permute-done | bytes 589856 | tf_op jit(solution)/shard_map/ppermute | solution.py:54
  135.7 16.9 %shard_map.264 = (bf16[1024,3072]{1,0:T(8,128)(2,1)}, bf16[1024,768]{1,0:T(8,128)(2,1)}, bf16[1024,768]{1,0:T(8,128)(2,1)}, bf16[768,256]{1,0:T(8,128)(2,1)}, f3...) custom-call(s32[4,16]{1,0:T(4,128)} %add_add_fusion.flags, bf16[1024,768]{1,0:T(8,128)(2,1)} %x.17, ...), custom_call_target="tpu_custom_call" | custom-call | flops 10000000000 | bytes 20000000 | tf_op jit(solution)/shard_map/pallas_call | solution.py:661
  157.8 3.6 collective-permute-done.16
  161.6 9.2 %shard_map.263 = (bf16[1024,3072]{1,0:T(8,128)(2,1)}, bf16[1024,768]{1,0:T(8,128)(2,1)}, bf16[1024,384]{1,0:T(8,128)(2,1)}) custom-call(s32[4,16]{1,0:T(4,128)} %add_add_fusion.flags, bf16[1024,768]{1,0:T(8,128)(2,1)} %x.17, bf16[768,768]{1,0:T(8,128)(2,1)} %get-tuple-element.97.weight, f32[1,768]{1,0:T(1,128)} %slice.90.bias, ...), custom_call_target="tpu_custom_call" | custom-call | flops 6000000000 | bytes 20000000 | tf_op jit(solution)/shard_map/pallas_call | solution.py:693
  170.9 9.1 %collective-permute-start.18 = (bf16[56,256]{1,0:T(8,128)(2,1)S(1)}, bf16[56,256]{1,0:T(8,128)(2,1)S(1)}, u32[]{:S(2)}, u32[]{:S(2)}) collective-permute-start(bf16[56,256]{1,0:T(8,128)(2,1)S(1)} %dynamic-slice_bitcast_fusion.17), channel_id=1, source_target_pairs={{0,16},{2,18},{4,20},{6,22},{8,24},{10,26},{12,28},{14,30},{16,0},... | collective-permute-start | bytes 86024 | tf_op jit(solution)/shard_map/ppermute | solution.py:50
  187.1 3.9 collective-permute-done.20
  199.0 45.5 %shard_map.265 = (bf16[1024,768]{1,0:T(8,128)(2,1)}, f32[1024,768]{1,0:T(8,128)}, f32[1024,768]{1,0:T(8,128)}, f32[1024,128]{1,0:T(8,128)}, bf16[1024,768]{1,0:T...) custom-call(s32[4,16]{1,0:T(4,128)} %add_add_fusion.flags, ...), custom_call_target="tpu_custom_call" | custom-call | flops 30000001024 | bytes 20000000 | tf_op jit(solution)/shard_map/pallas_call | solution.py:714
  244.5 5.0 convolution_convert_fusion.1
  249.7 20.7 %shard_map.266 = (f32[1024,768]{1,0:T(8,128)}, bf16[1024,768]{1,0:T(8,128)(2,1)}, bf16[1024,1536]{1,0:T(8,128)(2,1)}, bf16[1024,384]{1,0:T(8,128)(2,1)}, f32[24,...) custom-call(s32[4,16]{1,0:T(4,128)} %add_add_fusion.flags, ...), custom_call_target="tpu_custom_call" | custom-call | flops 6000000000 | bytes 20000000 | tf_op jit(solution)/shard_map/pallas_call | solution.py:757
  277.6 18.9 %shard_map.267 = (bf16[1024,768]{1,0:T(8,128)(2,1)}, f32[1024,768]{1,0:T(8,128)}, f32[8,768]{1,0:T(8,128)}) custom-call(s32[4,16]{1,0:T(4,128)} %add_add_fusion.flags, bf16[1024,1536]{1,0:T(8,128)(2,1)} %get-tuple-element.71.mixed, bf16[1024,3072]{1,0:T(8,128)(2,1)} %get-tuple-element.53.phi, bf16[1024,768]{1,0:T(8,128)(2,1)} %get-tuple-element.72.scaled, ...), custom_call_target="tpu_custom_call" | custom-call | flops 8000000000 | bytes 20000000 | tf_op jit(solution)/shard_map/pallas_call | solution.py:784
  302.0 9.5 %collective-permute-start.31 = (bf16[56,256]{1,0:T(8,128)(2,1)}, bf16[56,256]{1,0:T(8,128)(2,1)}, u32[]{:S(2)}, u32[]{:S(2)}) collective-permute-start(bf16[56,256]{1,0:T(8,128)(2,1)} %dynamic-slice_bitcast_fusion.16), channel_id=1, source_target_pairs={{0,16},{2,18},{4,20},{6,22},{8,24},{10,26},{12,28},{14,30},{16,0},... | collective-permute-start | bytes 86024 | tf_op jit(solution)/shard_map/ppermute | solution.py:50
  326.7 4.7 collective-permute-done.34
  331.5 6.3 %collective-permute-start.35 = (bf16[2,2,2,56,256]{4,3,2,1,0:T(8,128)(2,1)S(1)}, bf16[2,2,2,56,256]{4,3,2,1,0:T(8,128)(2,1)S(1)}, u32[]{:S(2)}, u32[]{:S(2)}) collective-permute-start(bf16[2,2,2,56,256]{4,3,2,1,0:T(8,128)(2,1)S(1)} %maximum_select_fusion.34), channel_id=1, source_target_pairs={{0,2},{2,0},{4,6},{6,4},{8,10},{10,8},{12,14},{14,12},{16,18},{18,... | collective-permute-start | bytes 688136 | tf_op jit(solution)/shard_map/ppermute | solution.py:50
  340.3 24.9 %shard_map.268 = (bf16[1024,1536]{1,0:T(8,128)(2,1)}, bf16[1024,768]{1,0:T(8,128)(2,1)}, f32[8,1536]{1,0:T(8,128)}) custom-call(s32[4,16]{1,0:T(4,128)} %add_add_fusion.flags, bf16[1024,3072]{1,0:T(8,128)(2,1)} %get-tuple-element.59.phi, bf16[1024,768]{1,0:T(8,128)(2,1)} %get-tuple-element.60.values, bf16[1024,768]{1,0:T(8,128)(2,1)} %get-tuple-element.61.scaled, ...), custom_call_target="tpu_custom_call" | custom-call | flops 12000000000 | bytes 20000000 | tf_op jit(solution)/shard_map/pallas_call | solution.py:805
  382.9 17.7 %collective-permute-start.43 = (f32[8,128]{1,0:T(8,128)S(1)}, f32[8,128]{1,0:T(8,128)S(1)}, u32[]{:S(2)}, u32[]{:S(2)}) collective-permute-start(f32[8,128]{1,0:T(8,128)S(1)} %fusion.40), channel_id=1, source_target_pairs={{0,16},{2,18},{4,20},{6,22},{8,24},{10,26},{12,28},{14,30},{16,0},... | collective-permute-start | bytes 12296 | tf_op jit(solution)/shard_map/ppermute | solution.py:50
  422.2 10.0 %collective-permute-done.49 = bf16[2,2,48,1536]{3,2,1,0:T(8,128)(2,1)S(1)} collective-permute-done((bf16[2,2,48,1536]{3,2,1,0:T(8,128)(2,1)S(1)}, bf16[2,2,48,1536]{3,2,1,0:T(8,128)(2,1)S(1)}, u32[]{:S(2)}, u32[]{:S(2)}) %collective-permute-start.49) | collective-permute-done | bytes 589856 | tf_op jit(solution)/shard_map/ppermute | solution.py:50
  432.7 12.0 %collective-permute-done.57 = bf16[2,2,96,768]{3,2,1,0:T(8,128)(2,1)S(1)} collective-permute-done((bf16[2,2,96,768]{3,2,1,0:T(8,128)(2,1)S(1)}, bf16[2,2,96,768]{3,2,1,0:T(8,128)(2,1)S(1)}, u32[]{:S(2)}, u32[]{:S(2)}) %collective-permute-start.57) | collective-permute-done | bytes 589856 | tf_op jit(solution)/shard_map/ppermute | solution.py:50
  450.6 6.4 %collective-permute-done.58 = bf16[2,96,768]{2,1,0:T(8,128)(2,1)S(1)} collective-permute-done((bf16[2,96,768]{2,1,0:T(8,128)(2,1)S(1)}, bf16[2,96,768]{2,1,0:T(8,128)(2,1)S(1)}, u32[]{:S(2)}, u32[]{:S(2)}) %collective-permute-start.58) | collective-permute-done | bytes 294944 | tf_op jit(solution)/shard_map/ppermute | solution.py:50
  460.2 8.7 %collective-permute-done.59 = bf16[96,768]{1,0:T(8,128)(2,1)S(1)} collective-permute-done((bf16[96,768]{1,0:T(8,128)(2,1)S(1)}, bf16[96,768]{1,0:T(8,128)(2,1)S(1)}, u32[]{:S(2)}, u32[]{:S(2)}) %collective-permute-start.59) | collective-permute-done | bytes 147488 | tf_op jit(solution)/shard_map/ppermute | solution.py:50
  469.0 6.2 %collective-permute-done.52 = bf16[48,1536]{1,0:T(8,128)(2,1)S(1)} collective-permute-done((bf16[48,1536]{1,0:T(8,128)(2,1)S(1)}, bf16[48,1536]{1,0:T(8,128)(2,1)S(1)}, u32[]{:S(2)}, u32[]{:S(2)}) %collective-permute-start.52) | collective-permute-done | bytes 147488 | tf_op jit(solution)/shard_map/ppermute | solution.py:50
  480.9 4.3 collective-permute-done.53
  486.9 4.6 collective-permute-done.61
  493.6 3.6 collective-permute-done.38
  497.4 4.2 collective-permute-done.54
  501.9 10.2 %collective-permute-done.62 = bf16[2,2,96,768]{3,2,0,1:T(8,128)(2,1)S(1)} collective-permute-done((bf16[2,2,96,768]{3,2,0,1:T(8,128)(2,1)S(1)}, bf16[2,2,96,768]{3,2,0,1:T(8,128)(2,1)S(1)}, u32[]{:S(2)}, u32[]{:S(2)}) %collective-permute-start.62) | collective-permute-done | bytes 589856 | tf_op jit(solution)/shard_map/ppermute | solution.py:50
  (367 shorter events, 177.3 us)
Async XLA Ops:
  4.8 25.8 %collective-permute-start.5 = (bf16[1,256]{1,0:T(2,128)(2,1)S(1)}, bf16[1,256]{1,0:T(2,128)(2,1)S(1)}, u32[]{:S(2)}, u32[]{:S(2)}) collective-permute-start(bf16[1,256]{1,0:T(2,128)(2,1)S(1)} %broadcast_in_dim.34), channel_id=1, source_target_pairs={{0,16},{2,18},{4,20},{6,22},{8,24},{10,26},{12,28},{14,30},{16,0},... | collective-permute-start | bytes 1544 | tf_op jit(solution)/shard_map/ppermute | solution.py:50
  9.5 27.5 %collective-permute-start.27 = (bf16[1,1536]{1,0:T(2,128)(2,1)S(1)}, bf16[1,1536]{1,0:T(2,128)(2,1)S(1)}, u32[]{:S(2)}, u32[]{:S(2)}) collective-permute-start(bf16[1,1536]{1,0:T(2,128)(2,1)S(1)} %convert_element_type.427), channel_id=1, source_target_pairs={{0,1},{1,0},{2,3},{3,2},{4,5},{5,4},{6,7},{7,6},{8,9},{9,8},{10,11... | collective-permute-start | bytes 9224 | tf_op jit(solution)/shard_map/ppermute | solution.py:54
  13.3 69.8 %collective-permute-start = (bf16[24,1536]{1,0:T(8,128)(2,1)}, bf16[24,1536]{1,0:T(8,128)(2,1)}, u32[]{:S(2)}, u32[]{:S(2)}) collective-permute-start(bf16[24,1536]{1,0:T(8,128)(2,1)} %get-tuple-element.113), channel_id=1, source_target_pairs={{0,16},{2,18},{4,20},{6,22},{8,24},{10,26},{12,28},{14,30},{16,0},... | collective-permute-start | bytes 221192 | tf_op jit(solution)/shard_map/ppermute | solution.py:50
  15.3 72.6 %collective-permute-start.10 = (bf16[24,1536]{1,0:T(8,128)(2,1)}, bf16[24,1536]{1,0:T(8,128)(2,1)}, u32[]{:S(2)}, u32[]{:S(2)}) collective-permute-start(bf16[24,1536]{1,0:T(8,128)(2,1)} %get-tuple-element.110), channel_id=1, source_target_pairs={{0,16},{2,18},{4,20},{6,22},{8,24},{10,26},{12,28},{14,30},{16,0},... | collective-permute-start | bytes 221192 | tf_op jit(solution)/shard_map/ppermute | solution.py:50
  19.2 112.7 %collective-permute-start.25 = (bf16[768,768]{1,0:T(8,128)(2,1)S(1)}, bf16[768,768]{1,0:T(8,128)(2,1)S(1)}, u32[]{:S(2)}, u32[]{:S(2)}) collective-permute-start(bf16[768,768]{1,0:T(8,128)(2,1)S(1)} %constant_dynamic-slice_fusion.8), channel_id=1, source_target_pairs={{0,1},{1,0},{2,3},{3,2},{4,5},{5,4},{6,7},{7,6},{8,9},{9,8},{10,11... | collective-permute-start | bytes 3538952 | tf_op jit(solution)/shard_map/ppermute | solution.py:54
  37.0 95.5 %collective-permute-start.23 = (bf16[384,1536]{1,0:T(8,128)(2,1)}, bf16[384,1536]{1,0:T(8,128)(2,1)S(1)}, u32[]{:S(2)}, u32[]{:S(2)}) collective-permute-start(bf16[384,1536]{1,0:T(8,128)(2,1)} %constant_dynamic-slice_fusion.9), channel_id=1, source_target_pairs={{0,1},{1,0},{2,3},{3,2},{4,5},{5,4},{6,7},{7,6},{8,9},{9,8},{10,11... | collective-permute-start | bytes 3538952 | tf_op jit(solution)/shard_map/ppermute | solution.py:54
  39.1 32.1 %collective-permute-start.8 = (bf16[2,2,2,1,256]{4,1,0,3,2:T(2,128)(2,1)S(1)}, bf16[2,2,2,1,256]{4,1,0,3,2:T(2,128)(2,1)S(1)}, u32[]{:S(2)}, u32[]{:S(2)}) collective-permute-start(bf16[2,2,2,1,256]{4,1,0,3,2:T(2,128)(2,1)S(1)} %broadcast_select_fusion.3), channel_id=1, source_target_pairs={{0,1},{1,0},{2,3},{3,2},{4,5},{5,4},{6,7},{7,6},{8,9},{9,8},{10,11... | collective-permute-start | bytes 12296 | tf_op jit(solution)/shard_map/ppermute | solution.py:54
  97.1 13.0 %collective-permute-start.2 = (bf16[2,2,24,1536]{3,2,0,1:T(8,128)(2,1)S(1)}, bf16[2,2,24,1536]{3,2,0,1:T(8,128)(2,1)S(1)}, u32[]{:S(2)}, u32[]{:S(2)}) collective-permute-start(bf16[2,2,24,1536]{3,2,0,1:T(8,128)(2,1)S(1)} %maximum_select_fusion.25), channel_id=1, source_target_pairs={{0,4},{2,6},{4,0},{6,2},{8,12},{10,14},{12,8},{14,10},{16,20},{18,... | collective-permute-start | bytes 884744 | tf_op jit(solution)/shard_map/ppermute | solution.py:50
  105.5 16.3 %collective-permute-start.13 = (bf16[2,2,2,24,1536]{4,3,0,1,2:T(8,128)(2,1)S(1)}, bf16[2,2,2,24,1536]{4,3,0,1,2:T(8,128)(2,1)S(1)}, u32[]{:S(2)}, u32[]{:S(2)}) collective-permute-start(bf16[2,2,2,24,1536]{4,3,0,1,2:T(8,128)(2,1)S(1)} %maximum_select_fusion.17), channel_id=1, source_target_pairs={{0,1},{1,0},{2,3},{3,2},{4,5},{5,4},{6,7},{7,6},{8,9},{9,8},{10,11... | collective-permute-start | bytes 1769480 | tf_op jit(solution)/shard_map/ppermute | solution.py:54
  110.2 20.1 %collective-permute-start.3 = (bf16[2,2,2,24,1536]{4,3,0,1,2:T(8,128)(2,1)S(1)}, bf16[2,2,2,24,1536]{4,3,0,1,2:T(8,128)(2,1)S(1)}, u32[]{:S(2)}, u32[]{:S(2)}) collective-permute-start(bf16[2,2,2,24,1536]{4,3,0,1,2:T(8,128)(2,1)S(1)} %maximum_select_fusion.15), channel_id=1, source_target_pairs={{0,1},{1,0},{2,3},{3,2},{4,5},{5,4},{6,7},{7,6},{8,9},{9,8},{10,11... | collective-permute-start | bytes 1769480 | tf_op jit(solution)/shard_map/ppermute | solution.py:54
  131.5 23.1 %collective-permute-start.4 = (bf16[2,2,2,2,24,1536]{5,4,0,1,2,3:T(8,128)(2,1)}, bf16[2,2,2,2,24,1536]{5,4,0,1,2,3:T(8,128)(2,1)S(1)}, u32[]{:S(2)}, u32[]{:S(2)}) collective-permute-start(bf16[2,2,2,2,24,1536]{5,4,0,1,2,3:T(8,128)(2,1)} %maximum_select_fusion.7), channel_id=1, source_target_pairs={{0,2},{2,0},{4,6},{6,4},{8,10},{10,8},{12,14},{14,12},{16,18},{18,... | collective-permute-start | bytes 3538952 | tf_op jit(solution)/shard_map/ppermute | solution.py:50
  131.9 52.9 %collective-permute-start.26 = (bf16[768,768]{1,0:T(8,128)(2,1)S(1)}, bf16[768,768]{1,0:T(8,128)(2,1)S(1)}, u32[]{:S(2)}, u32[]{:S(2)}) collective-permute-start(bf16[768,768]{1,0:T(8,128)(2,1)S(1)} %collective-permute-done.25), channel_id=1, source_target_pairs={{0,2},{2,0},{4,6},{6,4},{8,10},{10,8},{12,14},{14,12},{16,18},{18,... | collective-permute-start | bytes 3538952 | tf_op jit(solution)/shard_map/ppermute | solution.py:50
  132.5 47.5 %collective-permute-start.24 = (bf16[384,1536]{1,0:T(8,128)(2,1)S(1)}, bf16[384,1536]{1,0:T(8,128)(2,1)S(1)}, u32[]{:S(2)}, u32[]{:S(2)}) collective-permute-start(bf16[384,1536]{1,0:T(8,128)(2,1)S(1)} %collective-permute-done.23), channel_id=1, source_target_pairs={{0,2},{2,0},{4,6},{6,4},{8,10},{10,8},{12,14},{14,12},{16,18},{18,... | collective-permute-start | bytes 3538952 | tf_op jit(solution)/shard_map/ppermute | solution.py:50
  249.6 164.6 %collective-permute-start.48 = (bf16[2,2,2,48,1536]{4,3,2,1,0:T(8,128)(2,1)S(1)}, bf16[2,2,2,48,1536]{4,3,2,1,0:T(8,128)(2,1)}, u32[]{:S(2)}, u32[]{:S(2)}) collective-permute-start(bf16[2,2,2,48,1536]{4,3,2,1,0:T(8,128)(2,1)S(1)} %dynamic-slice_bitcast_fusion.1), channel_id=1, source_target_pairs={{0,2},{2,0},{4,6},{6,4},{8,10},{10,8},{12,14},{14,12},{16,18},{18,... | collective-permute-start | bytes 3538952 | tf_op jit(solution)/shard_map/ppermute | solution.py:50
  276.9 143.6 %collective-permute-start.56 = (bf16[2,2,2,96,768]{4,3,2,1,0:T(8,128)(2,1)}, bf16[2,2,2,96,768]{4,3,2,1,0:T(8,128)(2,1)}, u32[]{:S(2)}, u32[]{:S(2)}) collective-permute-start(bf16[2,2,2,96,768]{4,3,2,1,0:T(8,128)(2,1)} %dynamic-slice_bitcast_fusion), channel_id=1, source_target_pairs={{0,2},{2,0},{4,6},{6,4},{8,10},{10,8},{12,14},{14,12},{16,18},{18,... | collective-permute-start | bytes 3538952 | tf_op jit(solution)/shard_map/ppermute | solution.py:50
  277.5 19.0 %collective-permute-start.29 = (bf16[2,2,56,256]{3,2,0,1:T(8,128)(2,1)S(1)}, bf16[2,2,56,256]{3,2,0,1:T(8,128)(2,1)S(1)}, u32[]{:S(2)}, u32[]{:S(2)}) collective-permute-start(bf16[2,2,56,256]{3,2,0,1:T(8,128)(2,1)S(1)} %dynamic-slice_bitcast_fusion.11), channel_id=1, source_target_pairs={{0,4},{2,6},{4,0},{6,2},{8,12},{10,14},{12,8},{14,10},{16,20},{18,... | collective-permute-start | bytes 344072 | tf_op jit(solution)/shard_map/ppermute | solution.py:50
  302.0 13.0 %collective-permute-start.31 = (bf16[56,256]{1,0:T(8,128)(2,1)}, bf16[56,256]{1,0:T(8,128)(2,1)}, u32[]{:S(2)}, u32[]{:S(2)}) collective-permute-start(bf16[56,256]{1,0:T(8,128)(2,1)} %dynamic-slice_bitcast_fusion.16), channel_id=1, source_target_pairs={{0,16},{2,18},{4,20},{6,22},{8,24},{10,26},{12,28},{14,30},{16,0},... | collective-permute-start | bytes 86024 | tf_op jit(solution)/shard_map/ppermute | solution.py:50
  382.9 19.3 %collective-permute-start.43 = (f32[8,128]{1,0:T(8,128)S(1)}, f32[8,128]{1,0:T(8,128)S(1)}, u32[]{:S(2)}, u32[]{:S(2)}) collective-permute-start(f32[8,128]{1,0:T(8,128)S(1)} %fusion.40), channel_id=1, source_target_pairs={{0,16},{2,18},{4,20},{6,22},{8,24},{10,26},{12,28},{14,30},{16,0},... | collective-permute-start | bytes 12296 | tf_op jit(solution)/shard_map/ppermute | solution.py:50
  405.4 39.8 %collective-permute-start.36 = (bf16[2,2,2,24,3072]{4,3,0,1,2:T(8,128)(2,1)S(1)}, bf16[2,2,2,24,3072]{4,3,0,1,2:T(8,128)(2,1)S(1)}, u32[]{:S(2)}, u32[]{:S(2)}) collective-permute-start(bf16[2,2,2,24,3072]{4,3,0,1,2:T(8,128)(2,1)S(1)} %bitcast.381), channel_id=1, source_target_pairs={{0,2},{2,0},{4,6},{6,4},{8,10},{10,8},{12,14},{14,12},{16,18},{18,... | collective-permute-start | bytes 3538952 | tf_op jit(solution)/shard_map/ppermute | solution.py:50
  416.0 16.3 %collective-permute-start.49 = (bf16[2,2,48,1536]{3,2,1,0:T(8,128)(2,1)S(1)}, bf16[2,2,48,1536]{3,2,1,0:T(8,128)(2,1)S(1)}, u32[]{:S(2)}, u32[]{:S(2)}) collective-permute-start(bf16[2,2,48,1536]{3,2,1,0:T(8,128)(2,1)S(1)} %dynamic-slice_bitcast_fusion.3), channel_id=1, source_target_pairs={{0,4},{2,6},{4,0},{6,2},{8,12},{10,14},{12,8},{14,10},{16,20},{18,... | collective-permute-start | bytes 1769480 | tf_op jit(solution)/shard_map/ppermute | solution.py:50
  422.1 22.6 %collective-permute-start.57 = (bf16[2,2,96,768]{3,2,1,0:T(8,128)(2,1)S(1)}, bf16[2,2,96,768]{3,2,1,0:T(8,128)(2,1)S(1)}, u32[]{:S(2)}, u32[]{:S(2)}) collective-permute-start(bf16[2,2,96,768]{3,2,1,0:T(8,128)(2,1)S(1)} %dynamic-slice_bitcast_fusion.2), channel_id=1, source_target_pairs={{0,4},{2,6},{4,0},{6,2},{8,12},{10,14},{12,8},{14,10},{16,20},{18,... | collective-permute-start | bytes 1769480 | tf_op jit(solution)/shard_map/ppermute | solution.py:50
  432.5 15.0 %collective-permute-start.50 = (bf16[2,48,1536]{2,1,0:T(8,128)(2,1)S(1)}, bf16[2,48,1536]{2,1,0:T(8,128)(2,1)S(1)}, u32[]{:S(2)}, u32[]{:S(2)}) collective-permute-start(bf16[2,48,1536]{2,1,0:T(8,128)(2,1)S(1)} %dynamic-slice_bitcast_fusion.6), channel_id=1, source_target_pairs={{0,8},{2,10},{4,12},{6,14},{8,0},{10,2},{12,4},{14,6},{16,24},{18,... | collective-permute-start | bytes 884744 | tf_op jit(solution)/shard_map/ppermute | solution.py:50
  444.9 12.1 %collective-permute-start.58 = (bf16[2,96,768]{2,1,0:T(8,128)(2,1)S(1)}, bf16[2,96,768]{2,1,0:T(8,128)(2,1)S(1)}, u32[]{:S(2)}, u32[]{:S(2)}) collective-permute-start(bf16[2,96,768]{2,1,0:T(8,128)(2,1)S(1)} %dynamic-slice_bitcast_fusion.5), channel_id=1, source_target_pairs={{0,8},{2,10},{4,12},{6,14},{8,0},{10,2},{12,4},{14,6},{16,24},{18,... | collective-permute-start | bytes 884744 | tf_op jit(solution)/shard_map/ppermute | solution.py:50
  445.7 32.9 %collective-permute-start.37 = (bf16[2,2,24,3072]{3,2,0,1:T(8,128)(2,1)S(1)}, bf16[2,2,24,3072]{3,2,0,1:T(8,128)(2,1)S(1)}, u32[]{:S(2)}, u32[]{:S(2)}) collective-permute-start(bf16[2,2,24,3072]{3,2,0,1:T(8,128)(2,1)S(1)} %dynamic-slice_bitcast_fusion.4), channel_id=1, source_target_pairs={{0,4},{2,6},{4,0},{6,2},{8,12},{10,14},{12,8},{14,10},{16,20},{18,... | collective-permute-start | bytes 1769480 | tf_op jit(solution)/shard_map/ppermute | solution.py:50
  457.1 11.8 %collective-permute-start.59 = (bf16[96,768]{1,0:T(8,128)(2,1)S(1)}, bf16[96,768]{1,0:T(8,128)(2,1)S(1)}, u32[]{:S(2)}, u32[]{:S(2)}) collective-permute-start(bf16[96,768]{1,0:T(8,128)(2,1)S(1)} %dynamic-slice_bitcast_fusion.8), channel_id=1, source_target_pairs={{0,16},{2,18},{4,20},{6,22},{8,24},{10,26},{12,28},{14,30},{16,0},... | collective-permute-start | bytes 442376 | tf_op jit(solution)/shard_map/ppermute | solution.py:50
  458.0 17.2 %collective-permute-start.52 = (bf16[48,1536]{1,0:T(8,128)(2,1)S(1)}, bf16[48,1536]{1,0:T(8,128)(2,1)S(1)}, u32[]{:S(2)}, u32[]{:S(2)}) collective-permute-start(bf16[48,1536]{1,0:T(8,128)(2,1)S(1)} %fusion.21), channel_id=1, source_target_pairs={{0,16},{2,18},{4,20},{6,22},{8,24},{10,26},{12,28},{14,30},{16,0},... | collective-permute-start | bytes 442376 | tf_op jit(solution)/shard_map/ppermute | solution.py:50
  478.3 13.2 %collective-permute-start.61 = (bf16[2,96,768]{2,1,0:T(8,128)(2,1)S(1)}, bf16[2,96,768]{2,1,0:T(8,128)(2,1)S(1)}, u32[]{:S(2)}, u32[]{:S(2)}) collective-permute-start(bf16[2,96,768]{2,1,0:T(8,128)(2,1)S(1)} %maximum_select_fusion.31), channel_id=1, source_target_pairs={{0,8},{2,10},{4,12},{6,14},{8,0},{10,2},{12,4},{14,6},{16,24},{18,... | collective-permute-start | bytes 884744 | tf_op jit(solution)/shard_map/ppermute | solution.py:50
  478.8 18.4 %collective-permute-start.38 = (bf16[2,24,3072]{2,1,0:T(8,128)(2,1)S(1)}, bf16[2,24,3072]{2,1,0:T(8,128)(2,1)S(1)}, u32[]{:S(2)}, u32[]{:S(2)}) collective-permute-start(bf16[2,24,3072]{2,1,0:T(8,128)(2,1)S(1)} %dynamic-slice_bitcast_fusion.7), channel_id=1, source_target_pairs={{0,8},{2,10},{4,12},{6,14},{8,0},{10,2},{12,4},{14,6},{16,24},{18,... | collective-permute-start | bytes 884744 | tf_op jit(solution)/shard_map/ppermute | solution.py:50
  485.3 16.3 %collective-permute-start.54 = (bf16[2,2,48,1536]{3,2,0,1:T(8,128)(2,1)S(1)}, bf16[2,2,48,1536]{3,2,0,1:T(8,128)(2,1)S(1)}, u32[]{:S(2)}, u32[]{:S(2)}) collective-permute-start(bf16[2,2,48,1536]{3,2,0,1:T(8,128)(2,1)S(1)} %maximum_select_fusion.19), channel_id=1, source_target_pairs={{0,4},{2,6},{4,0},{6,2},{8,12},{10,14},{12,8},{14,10},{16,20},{18,... | collective-permute-start | bytes 1769480 | tf_op jit(solution)/shard_map/ppermute | solution.py:50
  491.6 20.5 %collective-permute-start.62 = (bf16[2,2,96,768]{3,2,0,1:T(8,128)(2,1)S(1)}, bf16[2,2,96,768]{3,2,0,1:T(8,128)(2,1)S(1)}, u32[]{:S(2)}, u32[]{:S(2)}) collective-permute-start(bf16[2,2,96,768]{3,2,0,1:T(8,128)(2,1)S(1)} %maximum_select_fusion.21), channel_id=1, source_target_pairs={{0,4},{2,6},{4,0},{6,2},{8,12},{10,14},{12,8},{14,10},{16,20},{18,... | collective-permute-start | bytes 1769480 | tf_op jit(solution)/shard_map/ppermute | solution.py:50
  497.3 15.1 %collective-permute-start.39 = (bf16[24,3072]{1,0:T(8,128)(2,1)S(1)}, bf16[24,3072]{1,0:T(8,128)(2,1)S(1)}, u32[]{:S(2)}, u32[]{:S(2)}) collective-permute-start(bf16[24,3072]{1,0:T(8,128)(2,1)S(1)} %dynamic-slice_bitcast_fusion.10), channel_id=1, source_target_pairs={{0,16},{2,18},{4,20},{6,22},{8,24},{10,26},{12,28},{14,30},{16,0},... | collective-permute-start | bytes 442376 | tf_op jit(solution)/shard_map/ppermute | solution.py:50
  501.8 12.4 %collective-permute-start.55 = (bf16[2,2,2,48,1536]{4,3,0,1,2:T(8,128)(2,1)S(1)}, bf16[2,2,2,48,1536]{4,3,0,1,2:T(8,128)(2,1)S(1)}, u32[]{:S(2)}, u32[]{:S(2)}) collective-permute-start(bf16[2,2,2,48,1536]{4,3,0,1,2:T(8,128)(2,1)S(1)} %maximum_select_fusion.11), channel_id=1, source_target_pairs={{0,2},{2,0},{4,6},{6,4},{8,10},{10,8},{12,14},{14,12},{16,18},{18,... | collective-permute-start | bytes 3538952 | tf_op jit(solution)/shard_map/ppermute | solution.py:50
  (49 other events, 352.1 us)
